TPU v7x, 32 devices: a whole 2x2x4 slice. The times are simulated.
32 devices in a mesh: grp: 2 (over y), gx: 4 (over z), gy: 4 (over x, core).
Axes of the slice: x: 2, y: 2, z: 4, core: 2. Of those that a mesh axis runs over, the one named last changes fastest.
Arguments:
- latents: bfloat16 [8, 4, 512, 128], P(('grp', 'gx'), 'gy'), parts along dimension 0, may hold values from -6 to 6
- edge_latents: bfloat16 [8, 4, 24, 256, 128], P(('grp', 'gx'), 'gy'), parts along dimension 0, may hold values from -6 to 6
- pair_send: int32 [8, 4, 24], P(('grp', 'gx'), 'gy'), parts along dimension 0, may hold values from 0 to 8, as said below
- pair_count: int32 [8, 4], P(('grp', 'gx'), 'gy'), parts along dimension 0, may hold values from 1 to 24, as said below
- edge_send: int32 [8, 4, 24, 256], P(('grp', 'gx'), 'gy'), parts along dimension 0, may hold values from 0 to 511
- edge_recv: int32 [8, 4, 24, 256], P(('grp', 'gx'), 'gy'), parts along dimension 0, may hold values from 0 to 511
- edge_w1: bfloat16 [384, 128], replicated, may hold values from -0.3125 to 0.3125
- edge_w2: bfloat16 [128, 128], replicated, may hold values from -0.5 to 0.5
- node_w1: bfloat16 [256, 128], replicated, may hold values from -0.375 to 0.375
- node_w2: bfloat16 [128, 128], replicated, may hold values from -0.5 to 0.5
- node_ct: bfloat16 [8, 4, 512, 128], P(('grp', 'gx'), 'gy'), parts along dimension 0, may hold values from -6 to 6
Outputs:
- node_out: bfloat16 [8, 4, 512, 128], P(('grp', 'gx'), 'gy'), parts along dimension 0
- node_grad: float32 [8, 4, 512, 128], P(('grp', 'gx'), 'gy'), parts along dimension 0
- grad_edge_w1: float32 [768, 128], P('grp'), parts along dimension 0
- grad_edge_w2: float32 [256, 128], P('grp'), parts along dimension 0
- grad_node_w1: float32 [512, 128], P('grp'), parts along dimension 0
- grad_node_w2: float32 [256, 128], P('grp'), parts along dimension 0
There are 2 independent parts, one for each index of `grp`. A program takes and returns all parts, laid end to end along the dimension named above; an argument that names none is the same for every part. Nothing has to cross between parts.
Inputs may be any that keep to these rules, and one draw needn't show every extreme that they name: `pair_send`: A slot's value s names the neighbour block at offsets (s // 3 - 1, s % 3 - 1) from its own column; that block lies inside the grid. `pair_count`: slots from this count on are padding. In every draw some device column uses all 24 slots.
All inputs are finite; a program needn't handle non-finite values.
Results may differ from a plain program's by a relative error of at most 0.0079.
Values may be sent and summed in bfloat16 or wider, within the bound.
A program may use at most 64 MiB of HBM per device.

v0:
```python
import math

import jax
import jax.numpy as jnp
from jax import lax
from jax.sharding import PartitionSpec as P

EPSILON = 1e-05


def with_halo(block, sides, width):
    for axis, dim in sides:
        count = lax.axis_size(axis)
        forward = [(i, i + 1) for i in range(count - 1)]
        backward = [(target, source) for source, target in forward]
        low = lax.ppermute(
            lax.slice_in_dim(block, block.shape[dim] - width, None, axis=dim), axis, forward
        )
        high = lax.ppermute(lax.slice_in_dim(block, 0, width, axis=dim), axis, backward)
        block = jnp.concatenate([low, block, high], axis=dim)
    return block


def passed_along(value, axis, steps):
    count = lax.axis_size(axis)
    initial, last = (max(0, -steps), min(count, count - steps))
    return lax.ppermute(value, axis, [(source, source + steps) for source in range(initial, last)])


def normalize(values):
    centre = jnp.mean(values, axis=-1, keepdims=True)
    shifted = values - centre
    inverse_std = lax.rsqrt(jnp.mean(shifted * shifted, axis=-1, keepdims=True) + EPSILON)
    return shifted * inverse_std


def normalize_back(values, upstream):
    centre = jnp.mean(values, axis=-1, keepdims=True)
    shifted = values - centre
    inverse_std = lax.rsqrt(jnp.mean(shifted * shifted, axis=-1, keepdims=True) + EPSILON)
    normed = shifted * inverse_std
    return inverse_std * (
        upstream
        - jnp.mean(upstream, axis=-1, keepdims=True)
        - normed * jnp.mean(upstream * normed, axis=-1, keepdims=True)
    )


def silu_slope(values):
    sigmoid = jax.nn.sigmoid(values)
    return sigmoid * (1.0 + values * (1.0 - sigmoid))


def contract_rows(left_side, right_side):
    return lax.dot_general(
        left_side, right_side, (((0,), (0,)), ((), ())), preferred_element_type=jnp.float32
    )


def contract_cols(left_side, right_side):
    return lax.dot_general(
        left_side, right_side, (((1,), (1,)), ((), ())), preferred_element_type=jnp.float32
    )


def edge_forward(edge_block, receivers, senders, edge_w1, edge_w2):
    stacked = jnp.concatenate([edge_block, receivers, senders], axis=-1)
    first_pre = jnp.dot(stacked, edge_w1, preferred_element_type=jnp.float32)
    first_act = jax.nn.silu(first_pre).astype(jnp.bfloat16)
    second_pre = jnp.dot(first_act, edge_w2, preferred_element_type=jnp.float32)
    return (stacked, first_pre, first_act, second_pre)


def edge_backward(stacked, first_pre, first_act, second_pre, upstream, edge_w1, edge_w2):
    feature_width = edge_w2.shape[1]
    grad_second = normalize_back(second_pre, upstream.astype(jnp.float32)).astype(jnp.bfloat16)
    slot_w2 = contract_rows(first_act, grad_second)
    grad_first = (contract_cols(grad_second, edge_w2) * silu_slope(first_pre)).astype(jnp.bfloat16)
    slot_w1 = contract_rows(stacked, grad_first)
    grad_inputs = contract_cols(grad_first, edge_w1[feature_width:]).astype(jnp.bfloat16)
    return (slot_w1, slot_w2, grad_inputs[:, :feature_width], grad_inputs[:, feature_width:])


def node_forward(latent_rows, aggregate, node_w1, node_w2):
    stacked = jnp.concatenate([latent_rows, aggregate], axis=-1)
    first_pre = jnp.dot(stacked, node_w1, preferred_element_type=jnp.float32)
    first_act = jax.nn.silu(first_pre).astype(jnp.bfloat16)
    second_pre = jnp.dot(first_act, node_w2, preferred_element_type=jnp.float32)
    updated = (latent_rows.astype(jnp.float32) + normalize(second_pre)).astype(jnp.bfloat16)
    return ((stacked, first_pre, first_act, second_pre), updated)


def node_backward(saved_parts, cotangent, node_w1, node_w2):
    stacked, first_pre, first_act, second_pre = saved_parts
    feature_width = node_w2.shape[1]
    upstream = cotangent.astype(jnp.float32)
    grad_second = normalize_back(second_pre, upstream).astype(jnp.bfloat16)
    grad_w2 = contract_rows(first_act, grad_second)
    grad_first = (contract_cols(grad_second, node_w2) * silu_slope(first_pre)).astype(jnp.bfloat16)
    grad_w1 = contract_rows(stacked, grad_first)
    grad_inputs = contract_cols(grad_first, node_w1)
    return (
        grad_w1,
        grad_w2,
        upstream + grad_inputs[:, :feature_width],
        grad_inputs[:, feature_width:].astype(jnp.bfloat16),
    )


def shards(
    latents,
    edge_latents,
    pair_send,
    pair_count,
    edge_send,
    edge_recv,
    edge_w1,
    edge_w2,
    node_w1,
    node_w2,
    node_ct,
):
    block_rows = latents.shape[2]
    feature_width = latents.shape[3]
    hidden_width = edge_w2.shape[0]
    own_rows = latents[0, 0]
    beside_all = with_halo(latents, (("gx", 0), ("gy", 1)), 1)
    beside_all = beside_all.reshape(9 * block_rows, feature_width)
    slot_edges = edge_latents[0, 0]
    sender_slot = pair_send[0, 0]
    used_slots = pair_count[0, 0]
    sender_ids = edge_send[0, 0]
    receiver_ids = edge_recv[0, 0]
    slot_total, pair_rows = sender_ids.shape
    positions = lax.broadcasted_iota(jnp.int32, (block_rows, pair_rows), 0)

    def selector(indices):
        return (positions == indices[None, :]).astype(jnp.bfloat16)

    def slot_inputs(slot_index):
        first_row = sender_slot[slot_index] * block_rows
        sender_block = lax.dynamic_slice_in_dim(beside_all, first_row, block_rows, 0)
        senders = jnp.take(sender_block, sender_ids[slot_index], axis=0)
        receivers = jnp.take(own_rows, receiver_ids[slot_index], axis=0)
        return edge_forward(slot_edges[slot_index], receivers, senders, edge_w1, edge_w2)

    def add_message(gathered, slot_index, outputs):
        message = normalize(outputs[3]).astype(jnp.bfloat16)
        return gathered + jnp.dot(
            selector(receiver_ids[slot_index]), message, preferred_element_type=jnp.float32
        )

    empty_rows = jnp.zeros((block_rows, feature_width), jnp.float32)
    buffers = (
        jnp.zeros((slot_total, pair_rows, 3 * feature_width), jnp.bfloat16),
        jnp.zeros((slot_total, pair_rows, hidden_width), jnp.float32),
        jnp.zeros((slot_total, pair_rows, hidden_width), jnp.bfloat16),
        jnp.zeros((slot_total, pair_rows, feature_width), jnp.float32),
    )

    def forward_slot(slot_index, running):
        outputs = slot_inputs(slot_index)
        kept = tuple(
            (
                lax.dynamic_update_index_in_dim(buffer, fresh_part, slot_index, 0)
                for buffer, fresh_part in zip(running[1], outputs)
            )
        )
        return (add_message(running[0], slot_index, outputs), kept)

    gathered, stored = lax.fori_loop(0, used_slots, forward_slot, (empty_rows, buffers))

    def recall(slot_index):
        return tuple(
            (lax.dynamic_index_in_dim(buffer, slot_index, 0, keepdims=False) for buffer in stored)
        )

    node_saved, updated = node_forward(own_rows, gathered.astype(jnp.bfloat16), node_w1, node_w2)
    grad_nw1, grad_nw2, grad_self, grad_aggregate = node_backward(
        node_saved, node_ct[0, 0], node_w1, node_w2
    )

    def backward_slot(slot_index, running):
        towards, local_sum, grad_w1, grad_w2 = running
        outputs = recall(slot_index)
        upstream = jnp.take(grad_aggregate, receiver_ids[slot_index], axis=0)
        slot_w1, slot_w2, to_receivers, to_senders = edge_backward(
            outputs[0], outputs[1], outputs[2], outputs[3], upstream, edge_w1, edge_w2
        )
        first_row = sender_slot[slot_index] * block_rows
        current = lax.dynamic_slice_in_dim(towards, first_row, block_rows, 0)
        current = current + jnp.dot(
            selector(sender_ids[slot_index]), to_senders, preferred_element_type=jnp.float32
        )
        towards = lax.dynamic_update_slice_in_dim(towards, current, first_row, 0)
        local_sum = local_sum + jnp.dot(
            selector(receiver_ids[slot_index]), to_receivers, preferred_element_type=jnp.float32
        )
        return (towards, local_sum, grad_w1 + slot_w1, grad_w2 + slot_w2)

    start_state = (
        jnp.zeros((9 * block_rows, feature_width), jnp.float32),
        empty_rows,
        jnp.zeros(edge_w1.shape, jnp.float32),
        jnp.zeros(edge_w2.shape, jnp.float32),
    )
    towards, local_sum, grad_w1, grad_w2 = lax.fori_loop(0, used_slots, backward_slot, start_state)
    pieces = towards.reshape(3, 3, block_rows, feature_width)
    row_span = lax.axis_size("gy")
    row_place = lax.axis_index("gy")
    incoming = pieces[1, 1]
    for across in range(3):
        for within in range(3):
            if across != 1 or within != 1:
                shift_gx = across - 1
                shift_gy = within - 1
                arrived = passed_along(
                    pieces[across, within].astype(jnp.bfloat16),
                    ("gx", "gy"),
                    shift_gx * row_span + shift_gy,
                ).astype(jnp.float32)
                inside = (row_place - shift_gy >= 0) & (row_place - shift_gy < row_span)
                incoming = incoming + jnp.where(inside, arrived, 0.0)
    node_grad = grad_self + local_sum + incoming
    summed = lax.psum((grad_w1, grad_w2, grad_nw1, grad_nw2), ("gx", "gy"))
    factor = 1.0 / math.sqrt(block_rows * lax.axis_size("gx") * lax.axis_size("gy"))
    return (
        updated[None, None],
        node_grad[None, None],
        summed[0] * factor,
        summed[1] * factor,
        summed[2] * factor,
        summed[3] * factor,
    )


def solution(mesh):
    placed = (
        P(("grp", "gx"), "gy", None, None),
        P(("grp", "gx"), "gy", None, None, None),
        P(("grp", "gx"), "gy", None),
        P(("grp", "gx"), "gy"),
        P(("grp", "gx"), "gy", None, None),
        P(("grp", "gx"), "gy", None, None),
        P(),
        P(),
        P(),
        P(),
        P(("grp", "gx"), "gy", None, None),
    )
    return jax.shard_map(
        shards,
        mesh=mesh,
        in_specs=placed,
        out_specs=(
            P(("grp", "gx"), "gy", None, None),
            P(("grp", "gx"), "gy", None, None),
            P("grp", None),
            P("grp", None),
            P("grp", None),
            P("grp", None),
        ),
        check_vma=False,
    )
```

profile of v0, /device:TPU:1, one launch (start us, length us, event | category | flops | bytes accessed | tf_op | source)
XLA Modules:
  0.0 693.8 jit_solution(8872834204654947943)
XLA Ops:
  7.2 4.0 collective-permute-start
  11.3 1.3 collective-permute-start.1
  14.7 2.5 collective-permute-done.1
  17.2 5.1 collective-permute-start.2
  22.3 1.9 collective-permute-start.3
  24.3 1.7 copy.29
  27.0 4.4 collective-permute-done.3
  31.6 2.8 broadcast_in_dim.70
  34.4 2.0 broadcast.110
  36.4 2.1 broadcast.110.clone
  38.8 139.3 %while.37 = (s32[]{:T(128)}, f32[512,128]{1,0:T(8,128)S(1)}, bf16[24,256,384]{2,1,0:T(8,128)(2,1)}, f32[24,256,128]{2,1,0:T(8,128)}, bf16[24,256,128]{2,1,0:T(8,...) while((s32[]{:T(128)}, f32[512,128]{1,0:T(8,128)S(1)}, ...), condition=%wide.region_3.5_spmd.clone, body=%wide.region_0.4_spmd.clone.sunk | while | flops 69114632 | bytes 3441965 | solution.py:171
  39.5 1.2 dynamic_slice.96
  45.0 1.7 bitcast_dynamic-update-slice_fusion.8
  50.1 1.2 dynamic_slice.96
  55.6 1.7 bitcast_dynamic-update-slice_fusion.8
  60.8 1.2 dynamic_slice.96
  66.3 1.7 bitcast_dynamic-update-slice_fusion.8
  71.5 1.2 dynamic_slice.96
  77.0 1.8 bitcast_dynamic-update-slice_fusion.8
  82.2 1.2 dynamic_slice.96
  87.7 1.8 bitcast_dynamic-update-slice_fusion.8
  98.4 1.7 bitcast_dynamic-update-slice_fusion.8
  109.0 1.8 bitcast_dynamic-update-slice_fusion.8
  114.2 1.2 dynamic_slice.96
  119.7 1.7 bitcast_dynamic-update-slice_fusion.8
  124.8 1.2 dynamic_slice.96
  130.3 1.7 bitcast_dynamic-update-slice_fusion.8
  141.0 1.7 bitcast_dynamic-update-slice_fusion.8
  146.2 1.2 dynamic_slice.96
  151.7 1.7 bitcast_dynamic-update-slice_fusion.8
  162.3 1.8 bitcast_dynamic-update-slice_fusion.8
  167.5 1.2 dynamic_slice.96
  173.0 1.7 bitcast_dynamic-update-slice_fusion.8
  178.3 1.4 multiply_convert_fusion.4
  183.9 141.7 %while.38 = (s32[]{:T(128)}, f32[4608,128]{1,0:T(8,128)S(1)}, f32[512,128]{1,0:T(8,128)S(1)}, f32[384,128]{1,0:T(8,128)S(1)}, f32[128,128]{1,0:T(8,128)S(1)}, /*...) while((s32[]{:T(128)}, f32[4608,128]{1,0:T(8,128)S(1)}, ...), condition=%wide.region_13.15_spmd.clone.clone, body=%wide.region_8.14_spmd.clone.clone.sunk | while | flops 127307272 | bytes 3935281 | solution.py:207
  190.1 1.2 dynamic_slice.102
  201.0 1.2 dynamic_slice.102
  211.8 1.2 dynamic_slice.102
  222.6 1.2 dynamic_slice.102
  233.5 1.2 dynamic_slice.102
  244.3 1.2 dynamic_slice.102
  255.2 1.2 dynamic_slice.102
  266.0 1.2 dynamic_slice.102
  276.9 1.2 dynamic_slice.102
  287.7 1.2 dynamic_slice.102
  298.6 1.2 dynamic_slice.102
  309.4 1.2 dynamic_slice.102
  320.3 1.2 dynamic_slice.102
  325.6 2.1 copy.39
  327.7 1.9 convert.14
  330.4 1.3 collective-permute-start.10
  331.7 1.3 collective-permute-start.11
  333.0 1.3 collective-permute-start.4
  334.3 1.3 collective-permute-start.5
  335.6 1.3 collective-permute-start.6
  338.8 233.0 %collective-permute-start.7 = (bf16[512,128]{0,1:T(8,128)(2,1)S(1)}, bf16[512,128]{0,1:T(8,128)(2,1)S(1)}, u32[]{:S(2)}, u32[]{:S(2)}) collective-permute-start(bf16[512,128]{0,1:T(8,128)(2,1)S(1)} %get-tuple-element.461), channel_id=1, source_target_pairs={{1,0},{2,1},{3,2},{4,3},{5,4},{6,5},{7,6},{8,7},{9,8},{10,9},{11,1... | collective-permute-start | bytes 393224 | tf_op jit(solution)/shard_map/ppermute | solution.py:27
  571.9 1.9 collective-permute-start.8
  573.8 5.5 collective-permute-start.9
  579.4 1.8 fusion.52
  583.3 97.5 %all-reduce.3.cloned.1.call-done = (f32[384,128]{1,0:T(8,128)}, f32[128,128]{1,0:T(8,128)}, f32[256,128]{1,0:T(8,128)}, f32[128,128]{1,0:T(8,128)}) async-done(((f32[384,128]{1,0:T(8,128)}, f32[128,128]{1,0:T(8,128)}, f32[256,128]{1,0:T(8,128)}, f32[128,128]{1,0:T(8,128)}), (f32[384,128]{1,0:T(8,128)}, f32[128,128]{1,0:T(8,128)}, f32[256,128]{1,0:T(8,128)}, ...) | async-done | bytes 458768 | tf_op jit(solution)/shard_map/psum | solution.py:225
  680.8 1.6 broadcast_multiply_fusion.4
  682.4 1.6 broadcast_multiply_fusion.5
  684.0 1.5 broadcast_multiply_fusion.6
  685.5 1.5 broadcast_multiply_fusion.7
  (615 shorter events, 206.2 us)
Async XLA Ops:
  7.2 171.1 %copy-start = (bf16[256,128]{1,0:T(8,128)(2,1)S(1)}, bf16[256,128]{1,0:T(8,128)(2,1)}, u32[]{:S(2)}) copy-start(bf16[256,128]{1,0:T(8,128)(2,1)} %param.25) | copy-start | bytes 196612
  7.2 673.6 %all-reduce.3.cloned.1.call-start = ((), (), s32[]{:S(2)}) async-start(), calls=%async_computation | async-start | bytes 917504 | tf_op jit(solution)/shard_map/psum | solution.py:225
  7.2 6.5 collective-permute-start
  11.3 5.9 collective-permute-start.1
  17.2 9.8 %collective-permute-start.2 = (bf16[3,1,512,128]{3,2,1,0:T(8,128)(2,1)S(1)}, bf16[3,1,512,128]{3,2,1,0:T(8,128)(2,1)S(1)}, u32[]{:S(2)}, u32[]{:S(2)}) collective-permute-start(bf16[3,1,512,128]{3,2,1,0:T(8,128)(2,1)S(1)} %constant_dynamic-update-slice_fusion), channel_id=1, source_target_pairs={{0,1},{1,2},{2,3},{4,5},{5,6},{6,7},{8,9},{9,10},{10,11},{12,13},{... | collective-permute-start | bytes 1179656 | tf_op jit(solution)/shard_map/ppermute | solution.py:16
  22.3 9.1 %collective-permute-start.3 = (bf16[3,1,512,128]{3,2,1,0:T(8,128)(2,1)S(1)}, bf16[3,1,512,128]{3,2,1,0:T(8,128)(2,1)S(1)}, u32[]{:S(2)}, u32[]{:S(2)}) collective-permute-start(bf16[3,1,512,128]{3,2,1,0:T(8,128)(2,1)S(1)} %constant_dynamic-update-slice_fusion), channel_id=1, source_target_pairs={{1,0},{2,1},{3,2},{5,4},{6,5},{7,6},{9,8},{10,9},{11,10},{13,12},{... | collective-permute-start | bytes 1179656 | tf_op jit(solution)/shard_map/ppermute | solution.py:19
  36.4 2.5 copy-start.1
  178.1 4.5 copy-start.4
  178.2 2.8 copy-start.6
  178.2 4.2 copy-start.16
  178.3 3.4 copy-start.13
  179.8 1.2 copy-start.11
  181.7 0.7 copy-start.8
  182.6 0.7 copy-start.15
  182.8 0.8 copy-start.5
  325.6 2.1 copy-start.2
  325.6 2.1 copy-start.3
  327.7 9.3 %slice-start = ((f32[512,256]{1,0:T(8,128)}), f32[512,128]{1,0:T(8,128)S(1)}, s32[]{:S(2)}) async-start(f32[512,256]{1,0:T(8,128)} %copy-done.5), calls=%async_computation.1 | async-start | bytes 524288 | tf_op jit(solution)/shard_map/slice | solution.py:105
  329.6 7.6 %copy-start.10 = (bf16[1,1,512,128]{2,3,1,0:T(8,128)(2,1)S(1)}, bf16[1,1,512,128]{2,3,1,0:T(8,128)(2,1)}, u32[]{:S(2)}) copy-start(bf16[1,1,512,128]{2,3,1,0:T(8,128)(2,1)} %get-tuple-element.465) | copy-start | bytes 393220
  329.6 8.4 %copy-start.9 = (bf16[512,128]{0,1:T(8,128)(2,1)S(1)}, bf16[512,128]{0,1:T(8,128)(2,1)}, u32[]{:S(2)}) copy-start(bf16[512,128]{0,1:T(8,128)(2,1)} %copy-done.8) | copy-start | bytes 393220
  329.6 8.4 %copy-start.12 = (bf16[512,128]{1,0:T(8,128)(2,1)S(1)}, bf16[512,128]{1,0:T(8,128)(2,1)}, u32[]{:S(2)}) copy-start(bf16[512,128]{1,0:T(8,128)(2,1)} %copy-done.11) | copy-start | bytes 393220
  329.6 249.8 %copy-start.7 = (bf16[1,1,512,128]{2,3,1,0:T(8,128)(2,1)S(1)}, bf16[1,1,512,128]{2,3,1,0:T(8,128)(2,1)}, u32[]{:S(2)}) copy-start(bf16[1,1,512,128]{2,3,1,0:T(8,128)(2,1)} %copy.29) | copy-start | bytes 393220
  329.6 249.7 %copy-start.14 = (bf16[512,128]{0,1:T(8,128)(2,1)S(1)}, bf16[512,128]{0,1:T(8,128)(2,1)}, u32[]{:S(2)}) copy-start(bf16[512,128]{0,1:T(8,128)(2,1)} %copy-done.13) | copy-start | bytes 393220
  330.4 8.4 %collective-permute-start.10 = (bf16[512,128]{0,1:T(8,128)(2,1)}, bf16[512,128]{0,1:T(8,128)(2,1)S(1)}, u32[]{:S(2)}, u32[]{:S(2)}) collective-permute-start(bf16[512,128]{0,1:T(8,128)(2,1)} %get-tuple-element.458), channel_id=1, source_target_pairs={{0,4},{1,5},{2,6},{3,7},{4,8},{5,9},{6,10},{7,11},{8,12},{9,13},{1... | collective-permute-start | bytes 393224 | tf_op jit(solution)/shard_map/ppermute | solution.py:27
  331.7 240.2 %collective-permute-start.11 = (bf16[512,128]{0,1:T(8,128)(2,1)S(1)}, bf16[512,128]{0,1:T(8,128)(2,1)S(1)}, u32[]{:S(2)}, u32[]{:S(2)}) collective-permute-start(bf16[512,128]{0,1:T(8,128)(2,1)S(1)} %get-tuple-element.457), channel_id=1, source_target_pairs={{0,5},{1,6},{2,7},{3,8},{4,9},{5,10},{6,11},{7,12},{8,13},{9,14},{... | collective-permute-start | bytes 393224 | tf_op jit(solution)/shard_map/ppermute | solution.py:27
  333.0 240.8 %collective-permute-start.4 = (bf16[512,128]{0,1:T(8,128)(2,1)S(1)}, bf16[512,128]{0,1:T(8,128)(2,1)S(1)}, u32[]{:S(2)}, u32[]{:S(2)}) collective-permute-start(bf16[512,128]{0,1:T(8,128)(2,1)S(1)} %get-tuple-element.456), channel_id=1, source_target_pairs={{5,0},{6,1},{7,2},{8,3},{9,4},{10,5},{11,6},{12,7},{13,8},{14,9},{... | collective-permute-start | bytes 393224 | tf_op jit(solution)/shard_map/ppermute | solution.py:27
  334.3 246.9 %collective-permute-start.5 = (bf16[512,128]{0,1:T(8,128)(2,1)S(1)}, bf16[512,128]{0,1:T(8,128)(2,1)S(1)}, u32[]{:S(2)}, u32[]{:S(2)}) collective-permute-start(bf16[512,128]{0,1:T(8,128)(2,1)S(1)} %get-tuple-element.463), channel_id=1, source_target_pairs={{4,0},{5,1},{6,2},{7,3},{8,4},{9,5},{10,6},{11,7},{12,8},{13,9},{1... | collective-permute-start | bytes 393224 | tf_op jit(solution)/shard_map/ppermute | solution.py:27
  335.6 245.6 %collective-permute-start.6 = (bf16[512,128]{0,1:T(8,128)(2,1)S(1)}, bf16[512,128]{0,1:T(8,128)(2,1)S(1)}, u32[]{:S(2)}, u32[]{:S(2)}) collective-permute-start(bf16[512,128]{0,1:T(8,128)(2,1)S(1)} %get-tuple-element.462), channel_id=1, source_target_pairs={{3,0},{4,1},{5,2},{6,3},{7,4},{8,5},{9,6},{10,7},{11,8},{12,9},{13... | collective-permute-start | bytes 393224 | tf_op jit(solution)/shard_map/ppermute | solution.py:27
  338.8 242.4 %collective-permute-start.7 = (bf16[512,128]{0,1:T(8,128)(2,1)S(1)}, bf16[512,128]{0,1:T(8,128)(2,1)S(1)}, u32[]{:S(2)}, u32[]{:S(2)}) collective-permute-start(bf16[512,128]{0,1:T(8,128)(2,1)S(1)} %get-tuple-element.461), channel_id=1, source_target_pairs={{1,0},{2,1},{3,2},{4,3},{5,4},{6,5},{7,6},{8,7},{9,8},{10,9},{11,1... | collective-permute-start | bytes 393224 | tf_op jit(solution)/shard_map/ppermute | solution.py:27
  571.9 9.3 %collective-permute-start.8 = (bf16[512,128]{0,1:T(8,128)(2,1)S(1)}, bf16[512,128]{0,1:T(8,128)(2,1)S(1)}, u32[]{:S(2)}, u32[]{:S(2)}) collective-permute-start(bf16[512,128]{0,1:T(8,128)(2,1)S(1)} %get-tuple-element.460), channel_id=1, source_target_pairs={{0,1},{1,2},{2,3},{3,4},{4,5},{5,6},{6,7},{7,8},{8,9},{9,10},{10,1... | collective-permute-start | bytes 393224 | tf_op jit(solution)/shard_map/ppermute | solution.py:27
  573.8 7.5 %collective-permute-start.9 = (bf16[512,128]{0,1:T(8,128)(2,1)S(1)}, bf16[512,128]{0,1:T(8,128)(2,1)S(1)}, u32[]{:S(2)}, u32[]{:S(2)}) collective-permute-start(bf16[512,128]{0,1:T(8,128)(2,1)S(1)} %get-tuple-element.459), channel_id=1, source_target_pairs={{0,3},{1,4},{2,5},{3,6},{4,7},{5,8},{6,9},{7,10},{8,11},{9,12},{10... | collective-permute-start | bytes 393224 | tf_op jit(solution)/shard_map/ppermute | solution.py:27
Sparse Core Ops, SparseCore 0:
  581.3 99.4 all-reduce.2
where the time goes:
time: 702 us; the launch traced here: 694 us
  starting transfers between devices  259 us (37%)
  local copies, waits for them, and re-layouts  123 us (18%)
  matrix products  108 us (15%)
  waiting for transfers between devices  106 us (15%)
  other arithmetic  46.2 us (7%)
  loops' own time  37.4 us (5%)
  between operations  14.5 us (2%)
    ppermute x8, starting transfers between devices, passed_along(): lax.ppermute(value, axis, [(source, source + steps) for source in range(i...  247 us
    psum x1, waiting for transfers between devices, shards(): summed = lax.psum((grad_w1, grad_w2, grad_nw1, grad_nw2), ('gx', 'gy'))  97.5 us
    dot_general x28, matrix products, contract_rows(): lax.dot_general(left_side, right_side, (((0,), (0,)), ((), ())), preferre...  31.6 us
    dot_general x28, matrix products, contract_cols(): lax.dot_general(left_side, right_side, (((1,), (1,)), ((), ())), preferre...  28.1 us
    dot_general x13, matrix products, edge_forward(): first_pre = jnp.dot(stacked, edge_w1, preferred_element_type=jnp.float32)  22.7 us
    another operation x1, loops' own time, shards(): lax.fori_loop(0, used_slots, backward_slot, start_state)  18.8 us
    another operation x1, loops' own time, shards(): lax.fori_loop(0, used_slots, forward_slot, (empty_rows, buffers))  18.6 us
    dynamic_slice x13, local copies, waits for them, and re-layouts, backward_slot(): first_row = sender_slot[slot_index] * block_rows  16.2 us
  transfers between devices with their start and end apart: 13, of which 5 were waited for; matrix products, arithmetic and copies ran while one was open for 1% of the time, Pallas kernels for 0%

commit v1 on v0

v1 whole, which is shorter than its diff:
```python
import functools
import math

import jax
import jax.numpy as jnp
from jax import lax
from jax.experimental import pallas as pl
from jax.experimental.pallas import tpu as pltpu
from jax.sharding import PartitionSpec as P

EPSILON = 1e-05
UNROLL = 2


def nn(a, b):
    return lax.dot_general(a, b, (((1,), (0,)), ((), ())), preferred_element_type=jnp.float32)


def nt(a, b):
    return lax.dot_general(a, b, (((1,), (1,)), ((), ())), preferred_element_type=jnp.float32)


def moments(values):
    centre = jnp.mean(values, axis=0, keepdims=True)
    shifted = values - centre
    inverse_std = lax.rsqrt(jnp.mean(shifted * shifted, axis=0, keepdims=True) + EPSILON)
    return shifted * inverse_std, inverse_std


def norm_back(normed, inverse_std, upstream):
    return inverse_std * (
        upstream
        - jnp.mean(upstream, axis=0, keepdims=True)
        - normed * jnp.mean(upstream * normed, axis=0, keepdims=True)
    )


def local_kernel(
    send_ref, count_ref, around_ref, edges_ref, sidx_ref, ridx_ref,
    w1_ref, w2_ref, nw1_ref, nw2_ref, own_ref, ct_ref,
    out_ref, self_ref, piece_ref, g1_ref, g2_ref, gn1_ref, gn2_ref,
    slope_s, act_s, hat_s, inv_s, w1t_s, agg_s, gagg_s, gr_s, gs_s, g1a_s,
):
    f32, b16 = jnp.float32, jnp.bfloat16
    slots, width = sidx_ref.shape
    features, rows = around_ref.shape[1:]
    count = count_ref[0]
    steps = lax.div(count + (UNROLL - 1), UNROLL)

    w1t_s[...] = w1_ref[...].astype(f32).T.astype(b16)
    w2t = w2_ref[...].astype(f32).T.astype(b16)
    agg_s[...] = jnp.zeros_like(agg_s)
    gr_s[...] = jnp.zeros_like(gr_s)
    gs_s[...] = jnp.zeros_like(gs_s)
    g1a_s[...] = jnp.zeros_like(g1a_s)
    g2_ref[...] = jnp.zeros_like(g2_ref)

    def place(index_ref, step, limit):
        parts = []
        for u in range(UNROLL):
            k = step * UNROLL + u
            index = index_ref[pl.ds(k, 1), :]
            if limit:
                index = jnp.where(k < count, index, rows)
            parts.append(index)
        index = jnp.concatenate(parts, axis=1)
        spot = lax.broadcasted_iota(jnp.int32, (rows, UNROLL * width), 0)
        return (spot == index).astype(f32).astype(b16)

    def forward(step, carry):
        at_recv = place(ridx_ref, step, True)
        at_send = place(sidx_ref, step, False)
        receivers = nn(around_ref[4], at_recv).astype(b16)
        senders = jnp.concatenate(
            [
                nn(
                    around_ref[send_ref[step * UNROLL + u]],
                    at_send[:, u * width : (u + 1) * width],
                ).astype(b16)
                for u in range(UNROLL)
            ],
            axis=1,
        )
        edge = edges_ref[pl.ds(step * UNROLL, UNROLL)].reshape(UNROLL * width, features)
        pre = nt(w1t_s[:, :features], edge) + nn(
            w1t_s[:, features:], jnp.concatenate([receivers, senders], axis=0)
        )
        sigmoid = 1.0 / (1.0 + jnp.exp(-pre))
        act = (pre * sigmoid).astype(b16)
        slope_s[step] = sigmoid * (1.0 + pre * (1.0 - sigmoid))
        act_s[step] = act
        normed, inverse_std = moments(nn(w2t, act))
        hat_s[step] = normed
        inv_s[step] = inverse_std
        agg_s[...] += nt(normed.astype(b16), at_recv)
        return carry

    lax.fori_loop(0, steps, forward, 0)

    own = around_ref[4]
    stacked = jnp.concatenate([own, agg_s[...].astype(b16)], axis=0)
    nw1t = nw1_ref[...].astype(f32).T.astype(b16)
    nw2t = nw2_ref[...].astype(f32).T.astype(b16)
    pre = nn(nw1t, stacked)
    sigmoid = 1.0 / (1.0 + jnp.exp(-pre))
    act = (pre * sigmoid).astype(b16)
    slope = sigmoid * (1.0 + pre * (1.0 - sigmoid))
    normed, inverse_std = moments(nn(nw2t, act))
    out_ref[...] = (own_ref[...].astype(f32) + normed.T).astype(b16)
    upstream = ct_ref[...].astype(f32).T
    grad_second = norm_back(normed, inverse_std, upstream).astype(b16)
    gn2_ref[...] = nt(act, grad_second)
    grad_first = (nn(nw2_ref[...], grad_second) * slope).astype(b16)
    gn1_ref[...] = nt(stacked, grad_first)
    grad_inputs = nn(nw1_ref[...], grad_first)
    self_ref[...] = upstream + grad_inputs[:features]
    gagg_s[...] = grad_inputs[features:].astype(b16)

    def backward(step, carry):
        at_recv = place(ridx_ref, step, True)
        at_send = place(sidx_ref, step, False)
        upstream = nn(gagg_s[...], at_recv)
        act = act_s[step]
        grad_second = norm_back(hat_s[step], inv_s[step], upstream).astype(b16)
        g2_ref[...] += nt(act, grad_second)
        grad_first = (nn(w2_ref[...], grad_second) * slope_s[step]).astype(b16)
        edge = edges_ref[pl.ds(step * UNROLL, UNROLL)].reshape(UNROLL * width, features)
        g1a_s[...] += nn(grad_first, edge)
        gr_s[...] += nt(grad_first, at_recv)
        for u in range(UNROLL):
            part = slice(u * width, (u + 1) * width)
            gs_s[send_ref[step * UNROLL + u]] += nt(grad_first[:, part], at_send[:, part])
        return carry

    lax.fori_loop(0, steps, backward, 0)

    to_recv = gr_s[...].astype(b16)
    g1_ref[:features] = g1a_s[...].T
    g1_ref[features : 2 * features] = nt(own, to_recv)
    self_ref[...] += nn(w1_ref[features : 2 * features], to_recv)
    total = jnp.zeros((features, features), f32)
    for b in range(9):
        to_send = gs_s[b].astype(b16)
        total += nt(around_ref[b], to_send)
        piece_ref[b] = nn(w1_ref[2 * features :], to_send).astype(b16)
    g1_ref[2 * features :] = total
    self_ref[...] += nn(w1_ref[2 * features :], gs_s[4].astype(b16))


def run_local(send, count, around, edges, sidx, ridx, w1, w2, nw1, nw2, own, ct):
    f32, b16 = jnp.float32, jnp.bfloat16
    rows, features = own.shape
    slots, width = sidx.shape
    steps = slots // UNROLL
    wide = UNROLL * width
    smem = pl.BlockSpec(memory_space=pltpu.SMEM)
    vmem = pl.BlockSpec(memory_space=pltpu.VMEM)
    shape = jax.ShapeDtypeStruct
    return pl.pallas_call(
        local_kernel,
        in_specs=[smem, smem] + [vmem] * 10,
        out_specs=[vmem] * 7,
        out_shape=[
            shape((rows, features), b16),
            shape((features, rows), f32),
            shape((9, features, rows), b16),
            shape((3 * features, features), f32),
            shape((features, features), f32),
            shape((2 * features, features), f32),
            shape((features, features), f32),
        ],
        scratch_shapes=[
            pltpu.VMEM((steps, features, wide), f32),
            pltpu.VMEM((steps, features, wide), b16),
            pltpu.VMEM((steps, features, wide), f32),
            pltpu.VMEM((steps, 1, wide), f32),
            pltpu.VMEM((features, 3 * features), b16),
            pltpu.VMEM((features, rows), f32),
            pltpu.VMEM((features, rows), b16),
            pltpu.VMEM((features, rows), f32),
            pltpu.VMEM((9, features, rows), f32),
            pltpu.VMEM((features, features), f32),
        ],
        compiler_params=pltpu.CompilerParams(vmem_limit_bytes=48 * 1024 * 1024),
    )(send, count, around, edges, sidx, ridx, w1, w2, nw1, nw2, own, ct)


def halo_permute(block):
    for axis, dim in (("gx", 0), ("gy", 1)):
        count = lax.axis_size(axis)
        forward = [(i, i + 1) for i in range(count - 1)]
        backward = [(target, source) for source, target in forward]
        low = lax.ppermute(block, axis, forward)
        high = lax.ppermute(block, axis, backward)
        block = jnp.concatenate([low, block, high], axis=dim)
    return block


def passed_along(value, axis, steps):
    count = lax.axis_size(axis)
    initial, last = (max(0, -steps), min(count, count - steps))
    return lax.ppermute(value, axis, [(source, source + steps) for source in range(initial, last)])


def return_permute(pieces, kept):
    row_span = lax.axis_size("gy")
    row_place = lax.axis_index("gy")
    incoming = kept
    for across in range(3):
        for within in range(3):
            if across != 1 or within != 1:
                shift_gx = across - 1
                shift_gy = within - 1
                arrived = passed_along(
                    pieces[3 * across + within],
                    ("gx", "gy"),
                    shift_gx * row_span + shift_gy,
                ).astype(jnp.float32)
                inside = (row_place - shift_gy >= 0) & (row_place - shift_gy < row_span)
                incoming = incoming + jnp.where(inside, arrived, 0.0)
    return incoming.T


def shards(
    latents, edge_latents, pair_send, pair_count, edge_send, edge_recv,
    edge_w1, edge_w2, node_w1, node_w2, node_ct,
):
    rows, features = latents.shape[2:]
    own = latents[0, 0]
    around = halo_permute(own.T[None, None]).reshape(9, features, rows)
    updated, kept, pieces, g1, g2, gn1, gn2 = run_local(
        pair_send[0, 0], pair_count[0], around, edge_latents[0, 0], edge_send[0, 0],
        edge_recv[0, 0], edge_w1, edge_w2, node_w1, node_w2, own, node_ct[0, 0],
    )
    node_grad = return_permute(pieces, kept)
    summed = lax.psum((g1, g2, gn1, gn2), ("gx", "gy"))
    factor = 1.0 / math.sqrt(rows * lax.axis_size("gx") * lax.axis_size("gy"))
    return (updated[None, None], node_grad[None, None]) + tuple(s * factor for s in summed)


def solution(mesh):
    block = P(("grp", "gx"), "gy")
    return jax.shard_map(
        shards,
        mesh=mesh,
        in_specs=(block,) * 6 + (P(),) * 4 + (block,),
        out_specs=(block, block) + (P("grp", None),) * 4,
        check_vma=False,
    )
```

time: 702 us -> 187 us (0.27); the launches traced: 694 us -> 187 us
  starting transfers between devices: 259 us -> 27.7 us
  local copies, waits for them, and re-layouts: 123 us -> 3.32 us
  matrix products: 108 us -> 0 us
  other arithmetic: 46.2 us -> 7.97 us
  loops' own time: 37.4 us -> 0 us
  Pallas kernels: 0 us -> 28.7 us
    ppermute x8, starting transfers between devices: 247 us -> 15.3 us  [passed_along(): lax.ppermute(value, axis, [(source, source + steps) for source in range(i...]
    dot_general x123 -> x0, matrix products: 108 us -> none  [the longest x28 31.6 us: contract_rows(): lax.dot_general(left_side, right_side, (((0,), (0,)), ((), ())), preferre...]
    dynamic_slice x78 -> x0, local copies, waits for them, and re-layouts: 52.6 us -> none  [the longest x13 16.2 us: backward_slot(): first_row = sender_slot[slot_index] * block_rows]
    another operation x2 -> x0, loops' own time: 37.4 us -> none  [the longest x1 18.8 us: shards(): lax.fori_loop(0, used_slots, backward_slot, start_state)]
    gather x39 -> x0, local copies, waits for them, and re-layouts: 33.3 us -> none  [the longest x13 11.1 us: slot_inputs(): receivers = jnp.take(own_rows, receiver_ids[slot_index], axis=0)]
    pallas_call x0 -> x1, Pallas kernels: none -> 28.7 us  [run_local(): pl.pallas_call(local_kernel, in_specs=[smem, smem] + [vmem] * 10, out_spe...]
    reduce_sum x55 -> x0, other arithmetic: 19 us -> none  [the longest x13 12.3 us: normalize_back(): centre = jnp.mean(values, axis=-1, keepdims=True)]
    squeeze x13 -> x1, local copies, waits for them, and re-layouts: 11.1 us -> 0.07 us  [return_permute(): pieces[3 * across + within]]
  transfers between devices with their start and end apart: 13 -> 13, of which waited for: 5 -> 6; matrix products, arithmetic and copies ran while one was open for 1% -> 1% of each run, Pallas kernels for 0% -> 0%
where the time goes in v1:
time: 187 us
  waiting for transfers between devices  104 us (56%)
  Pallas kernels  28.7 us (15%)
  starting transfers between devices  27.7 us (15%)
  between operations  15 us (8%)
  other arithmetic  7.97 us (4%)
  local copies, waits for them, and re-layouts  3.32 us (2%)
    psum x1, waiting for transfers between devices, shards(): summed = lax.psum((g1, g2, gn1, gn2), ('gx', 'gy'))  90.9 us
    pallas_call x1, Pallas kernels, run_local(): pl.pallas_call(local_kernel, in_specs=[smem, smem] + [vmem] * 10, out_spe...  28.7 us
    ppermute x8, starting transfers between devices, passed_along(): lax.ppermute(value, axis, [(source, source + steps) for source in range(i...  15.3 us
    ppermute x2, starting transfers between devices, halo_permute(): low = lax.ppermute(block, axis, forward)  9.15 us
    ppermute x2, waiting for transfers between devices, halo_permute(): high = lax.ppermute(block, axis, backward)  7.86 us
    mul x3, other arithmetic, shards(): s * factor  4.72 us
  transfers between devices with their start and end apart: 13, of which 6 were waited for; matrix products, arithmetic and copies ran while one was open for 1% of the time, Pallas kernels for 0%

profile of v1, /device:TPU:1, one launch (start us, length us, event | category | flops | bytes accessed | tf_op | source)
XLA Modules:
  0.0 186.6 jit_solution(6555648622924614902)
XLA Ops:
  7.2 0.0 all-reduce.3.cloned.1.call-start
  7.2 4.0 %collective-permute-start = (bf16[1,1,128,512]{2,3,1,0:T(8,128)(2,1)}, bf16[1,1,128,512]{2,3,1,0:T(8,128)(2,1)S(1)}, u32[]{:S(2)}, u32[]{:S(2)}) collective-permute-start(bf16[1,1,128,512]{2,3,1,0:T(8,128)(2,1)} %bitcast.35), channel_id=1, source_target_pairs={{0,4},{4,8},{8,12},{1,5},{5,9},{9,13},{2,6},{6,10},{10,14},{3,7},{... | collective-permute-start | bytes 393224 | tf_op jit(solution)/shard_map/ppermute | solution.py:193
  11.3 1.3 collective-permute-start.1
  12.6 1.2 collective-permute-done
  13.7 3.5 %collective-permute-done.1 = bf16[1,1,128,512]{2,3,1,0:T(8,128)(2,1)S(1)} collective-permute-done((bf16[1,1,128,512]{2,3,1,0:T(8,128)(2,1)}, bf16[1,1,128,512]{2,3,1,0:T(8,128)(2,1)S(1)}, u32[]{:S(2)}, u32[]{:S(2)}) %collective-permute-start.1) | collective-permute-done | bytes 131104 | tf_op jit(solution)/shard_map/ppermute | solution.py:194
  17.2 0.9 pad_maximum_fusion.1
  18.1 5.1 %collective-permute-start.2 = (bf16[3,1,128,512]{2,3,1,0:T(8,128)(2,1)S(1)}, bf16[3,1,128,512]{2,3,1,0:T(8,128)(2,1)S(1)}, u32[]{:S(2)}, u32[]{:S(2)}) collective-permute-start(bf16[3,1,128,512]{2,3,1,0:T(8,128)(2,1)S(1)} %pad_maximum_fusion.1), channel_id=1, source_target_pairs={{0,1},{1,2},{2,3},{4,5},{5,6},{6,7},{8,9},{9,10},{10,11},{12,13},{... | collective-permute-start | bytes 1179656 | tf_op jit(solution)/shard_map/ppermute | solution.py:193
  23.3 1.9 %collective-permute-start.3 = (bf16[3,1,128,512]{2,3,1,0:T(8,128)(2,1)S(1)}, bf16[3,1,128,512]{2,3,1,0:T(8,128)(2,1)S(1)}, u32[]{:S(2)}, u32[]{:S(2)}) collective-permute-start(bf16[3,1,128,512]{2,3,1,0:T(8,128)(2,1)S(1)} %pad_maximum_fusion.1), channel_id=1, source_target_pairs={{1,0},{2,1},{3,2},{5,4},{6,5},{7,6},{9,8},{10,9},{11,10},{13,12},{... | collective-permute-start | bytes 1179656 | tf_op jit(solution)/shard_map/ppermute | solution.py:194
  25.8 2.1 %collective-permute-done.2 = bf16[3,1,128,512]{2,3,1,0:T(8,128)(2,1)S(1)} collective-permute-done((bf16[3,1,128,512]{2,3,1,0:T(8,128)(2,1)S(1)}, bf16[3,1,128,512]{2,3,1,0:T(8,128)(2,1)S(1)}, u32[]{:S(2)}, u32[]{:S(2)}) %collective-permute-start.2) | collective-permute-done | bytes 393248 | tf_op jit(solution)/shard_map/ppermute | solution.py:193
  28.0 4.4 %collective-permute-done.3 = bf16[3,1,128,512]{2,3,1,0:T(8,128)(2,1)S(1)} collective-permute-done((bf16[3,1,128,512]{2,3,1,0:T(8,128)(2,1)S(1)}, bf16[3,1,128,512]{2,3,1,0:T(8,128)(2,1)S(1)}, u32[]{:S(2)}, u32[]{:S(2)}) %collective-permute-start.3) | collective-permute-done | bytes 393248 | tf_op jit(solution)/shard_map/ppermute | solution.py:194
  32.3 2.1 %pad_maximum_fusion = bf16[3,3,128,512]{2,3,1,0:T(8,128)(2,1)} fusion(bf16[3,1,128,512]{2,3,1,0:T(8,128)(2,1)S(1)} %collective-permute-done.3, bf16[1,1,128,512]{2,3,1,0:T(8,128)(2,1)S(1)} %collective-permute-done.1, bf16[1,1,128,512]{2,3,1,0:T(8,128)(2,1)} %bitcast.38, bf16[1,1,128,512]{2,3,1,0:T(8,128)(2,1)S(1)} %collective-permute-done, ...), kind=kLoop, calls=%fused_computation | loop fusion | flops 2359296 | bytes 2359296 | tf_op jit(solution)/shard_map/concatenate | solution.py:195
  34.4 0.0 copy-start
  34.4 0.0 copy-start.1
  34.4 0.0 copy-start.2
  34.4 0.0 copy-start.3
  34.4 0.0 copy-start.4
  34.5 0.0 copy-start.5
  34.5 0.0 copy-start.6
  34.5 0.0 copy-start.7
  34.5 0.0 copy-start.8
  34.5 1.7 copy.17.around_ref
  36.2 0.0 copy-done
  36.2 0.0 copy-done.1
  36.2 0.0 copy-done.2
  36.3 0.0 copy-done.3
  36.3 0.0 copy-done.4
  36.3 0.0 copy-done.5
  36.3 0.0 copy-done.6
  36.3 0.0 copy-done.7
  36.3 0.0 copy-done.8
  36.3 0.0 copy-start.9
  36.3 0.6 copy-done.9
  37.0 28.7 %shard_map.154 = (bf16[512,128]{1,0:T(8,128)(2,1)}, f32[128,512]{1,0:T(8,128)S(1)}, bf16[9,128,512]{2,1,0:T(8,128)(2,1)S(1)}, f32[384,128]{1,0:T(8,128)}, f32[12...) custom-call(s32[24]{0:T(128)S(1)} %bitcast.43, s32[1]{0:T(128)} %bitcast.33.count_ref, ...), custom_call_target="tpu_custom_call" | custom-call | tf_op jit(solution)/shard_map/pallas_call | solution.py:159
  65.7 0.1 slice_bitcast_fusion.7
  65.8 1.3 collective-permute-start.10
  67.1 1.3 collective-permute-start.11
  68.4 1.3 collective-permute-start.4
  69.7 1.3 collective-permute-start.5
  71.0 1.3 collective-permute-start.6
  72.3 0.0 collective-permute-done.10
  72.3 1.9 %collective-permute-start.7 = (bf16[128,512]{1,0:T(8,128)(2,1)S(1)}, bf16[128,512]{1,0:T(8,128)(2,1)S(1)}, u32[]{:S(2)}, u32[]{:S(2)}) collective-permute-start(bf16[128,512]{1,0:T(8,128)(2,1)S(1)} %get-tuple-element.35), channel_id=1, source_target_pairs={{1,0},{2,1},{3,2},{4,3},{5,4},{6,5},{7,6},{8,7},{9,8},{10,9},{11,1... | collective-permute-start | bytes 393224 | tf_op jit(solution)/shard_map/ppermute | solution.py:202
  74.2 0.0 collective-permute-done.11
  74.2 3.6 %collective-permute-start.8 = (bf16[128,512]{1,0:T(8,128)(2,1)S(1)}, bf16[128,512]{1,0:T(8,128)(2,1)S(1)}, u32[]{:S(2)}, u32[]{:S(2)}) collective-permute-start(bf16[128,512]{1,0:T(8,128)(2,1)S(1)} %get-tuple-element.34), channel_id=1, source_target_pairs={{0,1},{1,2},{2,3},{3,4},{4,5},{5,6},{6,7},{7,8},{8,9},{9,10},{10,1... | collective-permute-start | bytes 393224 | tf_op jit(solution)/shard_map/ppermute | solution.py:202
  77.9 0.0 collective-permute-done.4
  77.9 3.3 %collective-permute-start.9 = (bf16[128,512]{1,0:T(8,128)(2,1)S(1)}, bf16[128,512]{1,0:T(8,128)(2,1)S(1)}, u32[]{:S(2)}, u32[]{:S(2)}) collective-permute-start(bf16[128,512]{1,0:T(8,128)(2,1)S(1)} %get-tuple-element.33), channel_id=1, source_target_pairs={{0,3},{1,4},{2,5},{3,6},{4,7},{5,8},{6,9},{7,10},{8,11},{9,12},{10... | collective-permute-start | bytes 393224 | tf_op jit(solution)/shard_map/ppermute | solution.py:202
  81.2 0.0 all-reduce.3.cloned.1.call-update
  81.2 0.0 collective-permute-done.5
  81.2 0.0 collective-permute-done.6
  81.2 0.0 collective-permute-done.7
  81.2 0.0 collective-permute-done.8
  81.3 1.8 collective-permute-done.9
  83.1 0.2 add_bitcast_fusion
  83.3 0.8 copy.18
  84.2 90.9 %all-reduce.3.cloned.1.call-done = (f32[384,128]{1,0:T(8,128)}, f32[128,128]{1,0:T(8,128)}, f32[256,128]{1,0:T(8,128)}, f32[128,128]{1,0:T(8,128)}) async-done(((f32[384,128]{1,0:T(8,128)}, f32[128,128]{1,0:T(8,128)}, f32[256,128]{1,0:T(8,128)}, f32[128,128]{1,0:T(8,128)}), (f32[384,128]{1,0:T(8,128)}, f32[128,128]{1,0:T(8,128)}, f32[256,128]{1,0:T(8,128)}, ...) | async-done | bytes 458768 | tf_op jit(solution)/shard_map/psum | solution.py:236
  175.0 1.6 broadcast_multiply_fusion
  176.7 1.6 broadcast_multiply_fusion.1
  178.2 1.5 broadcast_multiply_fusion.2
Async XLA Ops:
  7.2 167.9 %all-reduce.3.cloned.1.call-start = ((), (), s32[]{:S(2)}) async-start(), calls=%async_computation | async-start | bytes 917504 | tf_op jit(solution)/shard_map/psum | solution.py:236
  7.2 6.5 %collective-permute-start = (bf16[1,1,128,512]{2,3,1,0:T(8,128)(2,1)}, bf16[1,1,128,512]{2,3,1,0:T(8,128)(2,1)S(1)}, u32[]{:S(2)}, u32[]{:S(2)}) collective-permute-start(bf16[1,1,128,512]{2,3,1,0:T(8,128)(2,1)} %bitcast.35), channel_id=1, source_target_pairs={{0,4},{4,8},{8,12},{1,5},{5,9},{9,13},{2,6},{6,10},{10,14},{3,7},{... | collective-permute-start | bytes 393224 | tf_op jit(solution)/shard_map/ppermute | solution.py:193
  11.3 5.9 %collective-permute-start.1 = (bf16[1,1,128,512]{2,3,1,0:T(8,128)(2,1)}, bf16[1,1,128,512]{2,3,1,0:T(8,128)(2,1)S(1)}, u32[]{:S(2)}, u32[]{:S(2)}) collective-permute-start(bf16[1,1,128,512]{2,3,1,0:T(8,128)(2,1)} %bitcast.36), channel_id=1, source_target_pairs={{4,0},{8,4},{12,8},{5,1},{9,5},{13,9},{6,2},{10,6},{14,10},{7,3},{... | collective-permute-start | bytes 393224 | tf_op jit(solution)/shard_map/ppermute | solution.py:194
  18.1 9.8 %collective-permute-start.2 = (bf16[3,1,128,512]{2,3,1,0:T(8,128)(2,1)S(1)}, bf16[3,1,128,512]{2,3,1,0:T(8,128)(2,1)S(1)}, u32[]{:S(2)}, u32[]{:S(2)}) collective-permute-start(bf16[3,1,128,512]{2,3,1,0:T(8,128)(2,1)S(1)} %pad_maximum_fusion.1), channel_id=1, source_target_pairs={{0,1},{1,2},{2,3},{4,5},{5,6},{6,7},{8,9},{9,10},{10,11},{12,13},{... | collective-permute-start | bytes 1179656 | tf_op jit(solution)/shard_map/ppermute | solution.py:193
  23.3 9.1 %collective-permute-start.3 = (bf16[3,1,128,512]{2,3,1,0:T(8,128)(2,1)S(1)}, bf16[3,1,128,512]{2,3,1,0:T(8,128)(2,1)S(1)}, u32[]{:S(2)}, u32[]{:S(2)}) collective-permute-start(bf16[3,1,128,512]{2,3,1,0:T(8,128)(2,1)S(1)} %pad_maximum_fusion.1), channel_id=1, source_target_pairs={{1,0},{2,1},{3,2},{5,4},{6,5},{7,6},{9,8},{10,9},{11,10},{13,12},{... | collective-permute-start | bytes 1179656 | tf_op jit(solution)/shard_map/ppermute | solution.py:194
  34.4 1.8 copy-start
  34.4 1.8 copy-start.1
  34.4 1.8 copy-start.2
  34.4 1.8 copy-start.3
  34.4 1.8 copy-start.4
  34.5 1.8 copy-start.5
  34.5 1.8 copy-start.6
  34.5 1.8 copy-start.7
  34.5 1.8 copy-start.8
  36.3 0.7 copy-start.9
  65.8 6.5 %collective-permute-start.10 = (bf16[128,512]{1,0:T(8,128)(2,1)S(1)}, bf16[128,512]{1,0:T(8,128)(2,1)S(1)}, u32[]{:S(2)}, u32[]{:S(2)}) collective-permute-start(bf16[128,512]{1,0:T(8,128)(2,1)S(1)} %get-tuple-element.32), channel_id=1, source_target_pairs={{0,4},{1,5},{2,6},{3,7},{4,8},{5,9},{6,10},{7,11},{8,12},{9,13},{1... | collective-permute-start | bytes 393224 | tf_op jit(solution)/shard_map/ppermute | solution.py:202
  67.1 7.1 %collective-permute-start.11 = (bf16[128,512]{1,0:T(8,128)(2,1)S(1)}, bf16[128,512]{1,0:T(8,128)(2,1)S(1)}, u32[]{:S(2)}, u32[]{:S(2)}) collective-permute-start(bf16[128,512]{1,0:T(8,128)(2,1)S(1)} %get-tuple-element.31), channel_id=1, source_target_pairs={{0,5},{1,6},{2,7},{3,8},{4,9},{5,10},{6,11},{7,12},{8,13},{9,14},{... | collective-permute-start | bytes 393224 | tf_op jit(solution)/shard_map/ppermute | solution.py:202
  68.4 9.5 %collective-permute-start.4 = (bf16[128,512]{1,0:T(8,128)(2,1)S(1)}, bf16[128,512]{1,0:T(8,128)(2,1)S(1)}, u32[]{:S(2)}, u32[]{:S(2)}) collective-permute-start(bf16[128,512]{1,0:T(8,128)(2,1)S(1)} %get-tuple-element.30), channel_id=1, source_target_pairs={{5,0},{6,1},{7,2},{8,3},{9,4},{10,5},{11,6},{12,7},{13,8},{14,9},{... | collective-permute-start | bytes 393224 | tf_op jit(solution)/shard_map/ppermute | solution.py:202
  69.7 11.5 %collective-permute-start.5 = (bf16[128,512]{1,0:T(8,128)(2,1)S(1)}, bf16[128,512]{1,0:T(8,128)(2,1)S(1)}, u32[]{:S(2)}, u32[]{:S(2)}) collective-permute-start(bf16[128,512]{1,0:T(8,128)(2,1)S(1)} %get-tuple-element.37), channel_id=1, source_target_pairs={{4,0},{5,1},{6,2},{7,3},{8,4},{9,5},{10,6},{11,7},{12,8},{13,9},{1... | collective-permute-start | bytes 393224 | tf_op jit(solution)/shard_map/ppermute | solution.py:202
  71.0 10.2 %collective-permute-start.6 = (bf16[128,512]{1,0:T(8,128)(2,1)S(1)}, bf16[128,512]{1,0:T(8,128)(2,1)S(1)}, u32[]{:S(2)}, u32[]{:S(2)}) collective-permute-start(bf16[128,512]{1,0:T(8,128)(2,1)S(1)} %get-tuple-element.36), channel_id=1, source_target_pairs={{3,0},{4,1},{5,2},{6,3},{7,4},{8,5},{9,6},{10,7},{11,8},{12,9},{13... | collective-permute-start | bytes 393224 | tf_op jit(solution)/shard_map/ppermute | solution.py:202
  72.3 8.9 %collective-permute-start.7 = (bf16[128,512]{1,0:T(8,128)(2,1)S(1)}, bf16[128,512]{1,0:T(8,128)(2,1)S(1)}, u32[]{:S(2)}, u32[]{:S(2)}) collective-permute-start(bf16[128,512]{1,0:T(8,128)(2,1)S(1)} %get-tuple-element.35), channel_id=1, source_target_pairs={{1,0},{2,1},{3,2},{4,3},{5,4},{6,5},{7,6},{8,7},{9,8},{10,9},{11,1... | collective-permute-start | bytes 393224 | tf_op jit(solution)/shard_map/ppermute | solution.py:202
  74.2 7.0 %collective-permute-start.8 = (bf16[128,512]{1,0:T(8,128)(2,1)S(1)}, bf16[128,512]{1,0:T(8,128)(2,1)S(1)}, u32[]{:S(2)}, u32[]{:S(2)}) collective-permute-start(bf16[128,512]{1,0:T(8,128)(2,1)S(1)} %get-tuple-element.34), channel_id=1, source_target_pairs={{0,1},{1,2},{2,3},{3,4},{4,5},{5,6},{6,7},{7,8},{8,9},{9,10},{10,1... | collective-permute-start | bytes 393224 | tf_op jit(solution)/shard_map/ppermute | solution.py:202
  77.9 5.2 %collective-permute-start.9 = (bf16[128,512]{1,0:T(8,128)(2,1)S(1)}, bf16[128,512]{1,0:T(8,128)(2,1)S(1)}, u32[]{:S(2)}, u32[]{:S(2)}) collective-permute-start(bf16[128,512]{1,0:T(8,128)(2,1)S(1)} %get-tuple-element.33), channel_id=1, source_target_pairs={{0,3},{1,4},{2,5},{3,6},{4,7},{5,8},{6,9},{7,10},{8,11},{9,12},{10... | collective-permute-start | bytes 393224 | tf_op jit(solution)/shard_map/ppermute | solution.py:202
Sparse Core Ops, SparseCore 0:
  81.3 93.6 all-reduce.2

commit v2 on v1

--- a/solution.py
+++ b/solution.py
@@ -36,10 +36,10 @@
 
 
 def local_kernel(
-    send_ref, count_ref, around_ref, edges_ref, sidx_ref, ridx_ref,
+    factor, send_ref, count_ref, around_ref, edges_ref, sidx_ref, ridx_ref,
     w1_ref, w2_ref, nw1_ref, nw2_ref, own_ref, ct_ref,
-    out_ref, self_ref, piece_ref, g1_ref, g2_ref, gn1_ref, gn2_ref,
-    slope_s, act_s, hat_s, inv_s, w1t_s, agg_s, gagg_s, gr_s, gs_s, g1a_s,
+    out_ref, self_ref, piece_ref, grads_ref,
+    slope_s, act_s, hat_s, inv_s, w1t_s, agg_s, gagg_s, gr_s, gs_s, g1a_s, g2_s,
 ):
     f32, b16 = jnp.float32, jnp.bfloat16
     slots, width = sidx_ref.shape
@@ -53,7 +53,7 @@
     gr_s[...] = jnp.zeros_like(gr_s)
     gs_s[...] = jnp.zeros_like(gs_s)
     g1a_s[...] = jnp.zeros_like(g1a_s)
-    g2_ref[...] = jnp.zeros_like(g2_ref)
+    g2_s[...] = jnp.zeros_like(g2_s)
 
     def place(index_ref, step, limit):
         parts = []
@@ -109,9 +109,9 @@
     out_ref[...] = (own_ref[...].astype(f32) + normed.T).astype(b16)
     upstream = ct_ref[...].astype(f32).T
     grad_second = norm_back(normed, inverse_std, upstream).astype(b16)
-    gn2_ref[...] = nt(act, grad_second)
+    grads_ref[6 * features : 7 * features] = nt(act, grad_second) * factor
     grad_first = (nn(nw2_ref[...], grad_second) * slope).astype(b16)
-    gn1_ref[...] = nt(stacked, grad_first)
+    grads_ref[4 * features : 6 * features] = nt(stacked, grad_first) * factor
     grad_inputs = nn(nw1_ref[...], grad_first)
     self_ref[...] = upstream + grad_inputs[:features]
     gagg_s[...] = grad_inputs[features:].astype(b16)
@@ -122,7 +122,7 @@
         upstream = nn(gagg_s[...], at_recv)
         act = act_s[step]
         grad_second = norm_back(hat_s[step], inv_s[step], upstream).astype(b16)
-        g2_ref[...] += nt(act, grad_second)
+        g2_s[...] += nt(act, grad_second)
         grad_first = (nn(w2_ref[...], grad_second) * slope_s[step]).astype(b16)
         edge = edges_ref[pl.ds(step * UNROLL, UNROLL)].reshape(UNROLL * width, features)
         g1a_s[...] += nn(grad_first, edge)
@@ -135,19 +135,22 @@
     lax.fori_loop(0, steps, backward, 0)
 
     to_recv = gr_s[...].astype(b16)
-    g1_ref[:features] = g1a_s[...].T
-    g1_ref[features : 2 * features] = nt(own, to_recv)
+    grads_ref[:features] = g1a_s[...].T * factor
+    grads_ref[features : 2 * features] = nt(own, to_recv) * factor
     self_ref[...] += nn(w1_ref[features : 2 * features], to_recv)
     total = jnp.zeros((features, features), f32)
     for b in range(9):
         to_send = gs_s[b].astype(b16)
         total += nt(around_ref[b], to_send)
         piece_ref[b] = nn(w1_ref[2 * features :], to_send).astype(b16)
-    g1_ref[2 * features :] = total
+    grads_ref[2 * features : 3 * features] = total * factor
+    grads_ref[3 * features : 4 * features] = g2_s[...] * factor
+    if grads_ref.shape[0] > 7 * features:
+        grads_ref[7 * features :] = jnp.zeros((grads_ref.shape[0] - 7 * features, features), f32)
     self_ref[...] += nn(w1_ref[2 * features :], gs_s[4].astype(b16))
 
 
-def run_local(send, count, around, edges, sidx, ridx, w1, w2, nw1, nw2, own, ct):
+def run_local(factor, padded, send, count, around, edges, sidx, ridx, w1, w2, nw1, nw2, own, ct):
     f32, b16 = jnp.float32, jnp.bfloat16
     rows, features = own.shape
     slots, width = sidx.shape
@@ -157,17 +160,14 @@
     vmem = pl.BlockSpec(memory_space=pltpu.VMEM)
     shape = jax.ShapeDtypeStruct
     return pl.pallas_call(
-        local_kernel,
+        functools.partial(local_kernel, factor),
         in_specs=[smem, smem] + [vmem] * 10,
-        out_specs=[vmem] * 7,
+        out_specs=[vmem] * 4,
         out_shape=[
             shape((rows, features), b16),
             shape((features, rows), f32),
             shape((9, features, rows), b16),
-            shape((3 * features, features), f32),
-            shape((features, features), f32),
-            shape((2 * features, features), f32),
-            shape((features, features), f32),
+            shape((padded, features), f32),
         ],
         scratch_shapes=[
             pltpu.VMEM((steps, features, wide), f32),
@@ -180,20 +180,207 @@
             pltpu.VMEM((features, rows), f32),
             pltpu.VMEM((9, features, rows), f32),
             pltpu.VMEM((features, features), f32),
+            pltpu.VMEM((features, features), f32),
         ],
         compiler_params=pltpu.CompilerParams(vmem_limit_bytes=48 * 1024 * 1024),
     )(send, count, around, edges, sidx, ridx, w1, w2, nw1, nw2, own, ct)
 
 
-def halo_permute(block):
-    for axis, dim in (("gx", 0), ("gy", 1)):
-        count = lax.axis_size(axis)
-        forward = [(i, i + 1) for i in range(count - 1)]
-        backward = [(target, source) for source, target in forward]
-        low = lax.ppermute(block, axis, forward)
-        high = lax.ppermute(block, axis, backward)
-        block = jnp.concatenate([low, block, high], axis=dim)
-    return block
+MESH = pl.DeviceIdType.MESH
+
+
+def neighbours():
+    p, q = lax.axis_index("gx"), lax.axis_index("gy")
+    found = []
+    for i in range(9):
+        if i != 4:
+            x, y = p + (i // 3 - 1), q + (i % 3 - 1)
+            inside = (x >= 0) & (x < lax.axis_size("gx")) & (y >= 0) & (y < lax.axis_size("gy"))
+            found.append((i, {"gx": x, "gy": y}, inside))
+    return found
+
+
+def greet(extra):
+    barrier = pltpu.get_barrier_semaphore()
+    total = jnp.int32(len(extra))
+    for _, where, inside in neighbours():
+        total = total + inside.astype(jnp.int32)
+
+        @pl.when(inside)
+        def _():
+            pl.semaphore_signal(barrier, inc=1, device_id=where, device_id_type=MESH)
+
+    for where in extra:
+        pl.semaphore_signal(barrier, inc=1, device_id=where, device_id_type=MESH)
+    pl.semaphore_wait(barrier, total)
+
+
+def remote(src, dst, send_sem, recv_sem, where):
+    return pltpu.make_async_remote_copy(
+        src_ref=src, dst_ref=dst, send_sem=send_sem, recv_sem=recv_sem,
+        device_id=where, device_id_type=MESH,
+    )
+
+
+def halo_kernel(own_ref, around_ref, mine_s, send_sem, recv_sem):
+    mine = own_ref[...].astype(jnp.float32).T.astype(jnp.bfloat16)
+    mine_s[...] = mine
+    around_ref[4] = mine
+    greet([])
+    for i, where, inside in neighbours():
+
+        @pl.when(inside)
+        def _():
+            remote(mine_s, around_ref.at[8 - i], send_sem.at[i], recv_sem.at[8 - i], where).start()
+
+        @pl.when(jnp.logical_not(inside))
+        def _():
+            around_ref[i] = jnp.zeros(mine.shape, mine.dtype)
+
+    for i, where, inside in neighbours():
+
+        @pl.when(inside)
+        def _():
+            remote(mine_s, around_ref.at[i], send_sem.at[i], recv_sem.at[i], where).wait()
+
+
+def run_halo(own):
+    rows, features = own.shape
+    vmem = pl.BlockSpec(memory_space=pltpu.VMEM)
+    return pl.pallas_call(
+        halo_kernel,
+        in_specs=[vmem],
+        out_specs=vmem,
+        out_shape=jax.ShapeDtypeStruct((9, features, rows), own.dtype),
+        scratch_shapes=[
+            pltpu.VMEM((features, rows), own.dtype),
+            pltpu.SemaphoreType.DMA((9,)),
+            pltpu.SemaphoreType.DMA((9,)),
+        ],
+        compiler_params=pltpu.CompilerParams(collective_id=0, has_side_effects=True),
+    )(own)
+
+
+def tail_kernel(
+    pieces_ref, kept_ref, grads_ref, node_ref, g1_ref, g2_ref, gn1_ref, gn2_ref,
+    back_s, acc_s, low_s, sum_s, low2_s, row_s, col_s, full_s,
+    send_h, recv_h, send_r, recv_r,
+):
+    f32, b16 = jnp.float32, jnp.bfloat16
+    p, q = lax.axis_index("gx"), lax.axis_index("gy")
+    nx, ny = lax.axis_size("gx"), lax.axis_size("gy")
+    padded, features = grads_ref.shape
+    big, small = padded // ny, padded // (nx * ny)
+    along_y = [(d, lax.rem(q + d, ny)) for d in range(1, ny)]
+    along_x = [(d, lax.rem(p + d, nx)) for d in range(1, nx)]
+
+    low_s[...] = grads_ref[...].astype(b16)
+    greet([{"gy": y} for _, y in along_y] + [{"gx": x} for _, x in along_x])
+
+    def rows_of(ref, start, size):
+        return ref.at[pl.ds(pl.multiple_of(start, size), size)]
+
+    scatter_y = [
+        remote(rows_of(low_s, y * big, big), row_s.at[d], send_r.at[0, d], recv_r.at[0, d], {"gy": y})
+        for d, y in along_y
+    ]
+    for copy in scatter_y:
+        copy.start()
+    for i, where, inside in neighbours():
+
+        @pl.when(inside)
+        def _():
+            remote(pieces_ref.at[i], back_s.at[8 - i], send_h.at[i], recv_h.at[8 - i], where).start()
+
+    total = grads_ref[pl.ds(pl.multiple_of(q * big, big), big), :]
+    for (d, _), copy in zip(along_y, scatter_y):
+        copy.wait_recv()
+        total = total + row_s[d].astype(f32)
+    sum_s[...] = total
+    low2_s[...] = total.astype(b16)
+    scatter_x = [
+        remote(rows_of(low2_s, x * small, small), col_s.at[d], send_r.at[1, d], recv_r.at[1, d], {"gx": x})
+        for d, x in along_x
+    ]
+    for copy in scatter_x:
+        copy.start()
+    total = sum_s[pl.ds(pl.multiple_of(p * small, small), small), :]
+    for (d, _), copy in zip(along_x, scatter_x):
+        copy.wait_recv()
+        total = total + col_s[d].astype(f32)
+    own_rows = rows_of(full_s, q * big + p * small, small)
+    own_rows[...] = total.astype(b16)
+    gather_x = [
+        remote(own_rows, own_rows, send_r.at[2, d], recv_r.at[2, d], {"gx": x}) for d, x in along_x
+    ]
+    for copy in gather_x:
+        copy.start()
+    for d, _ in along_x:
+        source = lax.rem(p + nx - d, nx)
+        theirs = rows_of(full_s, q * big + source * small, small)
+        remote(theirs, theirs, send_r.at[2, d], recv_r.at[2, d], {"gx": source}).wait_recv()
+    for copy in gather_x:
+        copy.wait_send()
+    own_big = rows_of(full_s, q * big, big)
+    gather_y = [
+        remote(own_big, own_big, send_r.at[3, d], recv_r.at[3, d], {"gy": y}) for d, y in along_y
+    ]
+    for copy in gather_y:
+        copy.start()
+
+    acc_s[...] = kept_ref[...]
+    for i, where, inside in neighbours():
+
+        @pl.when(inside)
+        def _():
+            remote(pieces_ref.at[i], back_s.at[i], send_h.at[i], recv_h.at[i], where).wait()
+            acc_s[...] += back_s[i].astype(f32)
+
+    node_ref[...] = acc_s[...].T
+    for d, _ in along_y:
+        source = lax.rem(q + ny - d, ny)
+        theirs = rows_of(full_s, source * big, big)
+        remote(theirs, theirs, send_r.at[3, d], recv_r.at[3, d], {"gy": source}).wait_recv()
+    g1_ref[...] = full_s[: 3 * features].astype(f32)
+    g2_ref[...] = full_s[3 * features : 4 * features].astype(f32)
+    gn1_ref[...] = full_s[4 * features : 6 * features].astype(f32)
+    gn2_ref[...] = full_s[6 * features : 7 * features].astype(f32)
+    for copy in scatter_y + scatter_x + gather_y:
+        copy.wait_send()
+
+
+def run_tail(pieces, kept, grads):
+    f32, b16 = jnp.float32, jnp.bfloat16
+    features, rows = kept.shape
+    nx, ny = lax.axis_size("gx"), lax.axis_size("gy")
+    padded = grads.shape[0]
+    big, small = padded // ny, padded // (nx * ny)
+    vmem = pl.BlockSpec(memory_space=pltpu.VMEM)
+    shape = jax.ShapeDtypeStruct
+    return pl.pallas_call(
+        tail_kernel,
+        in_specs=[vmem] * 3,
+        out_specs=[vmem] * 5,
+        out_shape=[shape((rows, features), f32)]
+        + [shape((n * features, features), f32) for n in (3, 1, 2, 1)],
+        scratch_shapes=[
+            pltpu.VMEM((9, features, rows), b16),
+            pltpu.VMEM((features, rows), f32),
+            pltpu.VMEM((padded, features), b16),
+            pltpu.VMEM((big, features), f32),
+            pltpu.VMEM((big, features), b16),
+            pltpu.VMEM((ny, big, features), b16),
+            pltpu.VMEM((nx, small, features), b16),
+            pltpu.VMEM((padded, features), b16),
+            pltpu.SemaphoreType.DMA((9,)),
+            pltpu.SemaphoreType.DMA((9,)),
+            pltpu.SemaphoreType.DMA((4, max(nx, ny))),
+            pltpu.SemaphoreType.DMA((4, max(nx, ny))),
+        ],
+        compiler_params=pltpu.CompilerParams(
+            collective_id=1, has_side_effects=True, vmem_limit_bytes=32 * 1024 * 1024
+        ),
+    )(pieces, kept, grads)
 
 
 def passed_along(value, axis, steps):
@@ -227,15 +414,23 @@
 ):
     rows, features = latents.shape[2:]
     own = latents[0, 0]
-    around = halo_permute(own.T[None, None]).reshape(9, features, rows)
-    updated, kept, pieces, g1, g2, gn1, gn2 = run_local(
-        pair_send[0, 0], pair_count[0], around, edge_latents[0, 0], edge_send[0, 0],
-        edge_recv[0, 0], edge_w1, edge_w2, node_w1, node_w2, own, node_ct[0, 0],
+    around = run_halo(own)
+    nx, ny = lax.axis_size("gx"), lax.axis_size("gy")
+    factor = 1.0 / math.sqrt(rows * nx * ny)
+    direct = nx * ny <= 16
+    unit = 16 * nx * ny if direct else 1
+    padded = -(-7 * features // unit) * unit
+    updated, kept, pieces, grads = run_local(
+        factor, padded, pair_send[0, 0], pair_count[0], around, edge_latents[0, 0],
+        edge_send[0, 0], edge_recv[0, 0], edge_w1, edge_w2, node_w1, node_w2, own, node_ct[0, 0],
     )
-    node_grad = return_permute(pieces, kept)
-    summed = lax.psum((g1, g2, gn1, gn2), ("gx", "gy"))
-    factor = 1.0 / math.sqrt(rows * lax.axis_size("gx") * lax.axis_size("gy"))
-    return (updated[None, None], node_grad[None, None]) + tuple(s * factor for s in summed)
+    if direct:
+        node_grad, *summed = run_tail(pieces, kept, grads)
+    else:
+        node_grad = return_permute(pieces, kept)
+        grads = lax.psum(grads, ("gx", "gy"))
+        summed = jnp.split(grads, (3 * features, 4 * features, 6 * features))
+    return (updated[None, None], node_grad[None, None]) + tuple(summed)
 
 
 def solution(mesh):

time: 187 us -> 71.4 us (0.38)
  waiting for transfers between devices: 104 us -> 0 us
  Pallas kernels: 28.7 us -> 63 us
  starting transfers between devices: 27.7 us -> 0 us
  between operations: 15 us -> 1.58 us
  other arithmetic: 7.97 us -> 0 us
  local copies, waits for them, and re-layouts: 3.32 us -> 6 us
    psum x1 -> x0, waiting for transfers between devices: 90.9 us -> none  [shards(): summed = lax.psum((g1, g2, gn1, gn2), ('gx', 'gy'))]
    pallas_call x1 -> x3, Pallas kernels: 28.7 us -> 63 us  [the longest x1 28.1 us: run_local(): pl.pallas_call(functools.partial(local_kernel, factor), in_specs=[smem, s...]
    ppermute x12 -> x0, starting transfers between devices: 27.7 us -> none  [the longest x8 15.3 us: passed_along(): lax.ppermute(value, axis, [(source, source + steps) for source in range(i...]
    ppermute x12 -> x0, waiting for transfers between devices: 13 us -> none  [the longest x2 7.86 us: halo_permute(): high = lax.ppermute(block, axis, backward)]
    mul x3 -> x0, other arithmetic: 4.72 us -> none  [shards(): s * factor]
    unnamed x21 -> x27, local copies, waits for them, and re-layouts: 1.53 us -> 6 us
    concatenate x2 -> x0, other arithmetic: 3.04 us -> none  [halo_permute(): block = jnp.concatenate([low, block, high], axis=dim)]
  transfers between devices with their start and end apart: 13 -> 0, of which waited for: 6 -> 0; matrix products, arithmetic and copies ran while one was open for 1% -> 0% of each run, Pallas kernels for 0% -> 0%
where the time goes in v2:
time: 71.4 us; the launch traced here: 70.6 us
  Pallas kernels  63 us (88%)
  local copies, waits for them, and re-layouts  6 us (8%)
  between operations  1.58 us (2%)
    pallas_call x1, Pallas kernels, run_local(): pl.pallas_call(functools.partial(local_kernel, factor), in_specs=[smem, s...  28.1 us
    pallas_call x1, Pallas kernels, run_tail(): pl.pallas_call(tail_kernel, in_specs=[vmem] * 3, out_specs=[vmem] * 5, ou...  21.5 us
    pallas_call x1, Pallas kernels, run_halo(): pl.pallas_call(halo_kernel, in_specs=[vmem], out_specs=vmem, out_shape=ja...  13.4 us
    unnamed x27, local copies, waits for them, and re-layouts  6 us

profile of v2, /device:TPU:1, one launch (start us, length us, event | category | flops | bytes accessed | tf_op | source)
XLA Modules:
  0.0 70.6 jit_solution(14751060009978919579)
XLA Ops:
  0.6 0.0 copy-start.3
  0.6 0.0 copy-start.7
  0.7 0.0 copy-start.5
  0.7 0.0 copy-start.6
  0.7 0.0 copy-start.4
  0.7 0.0 copy-start.9
  0.7 0.0 copy-start.8
  0.7 0.0 copy-start.10
  0.7 0.0 copy-start.2
  1.5 13.4 %shard_map.154.around_ref = bf16[9,128,512]{2,1,0:T(8,128)(2,1)} custom-call(bf16[512,128]{1,0:T(8,128)(2,1)} %bitcast.11), custom_call_target="tpu_custom_call" | custom-call | tf_op jit(solution)/shard_map/pallas_call | solution.py:250
  14.9 0.0 copy-done.3
  14.9 0.0 copy-done.7
  14.9 0.0 copy-done.5
  14.9 0.0 copy-done.6
  14.9 0.0 copy-done.4
  14.9 0.0 copy-done.9
  14.9 0.0 copy-done.8
  14.9 0.0 copy-done.10
  14.9 0.0 copy-done.2
  14.9 0.0 copy-start
  15.0 1.3 %copy-done = bf16[9,128,512]{2,1,0:T(8,128)(2,1)S(1)} copy-done((bf16[9,128,512]{2,1,0:T(8,128)(2,1)S(1)}, bf16[9,128,512]{2,1,0:T(8,128)(2,1)}, u32[]{:S(2)}) %copy-start) | copy-done | bytes 1179672
  16.2 0.0 copy-start.1
  16.2 1.4 %copy-done.1 = bf16[1,1,24,256,128]{4,3,2,1,0:T(8,128)(2,1)S(1)} copy-done((bf16[1,1,24,256,128]{4,3,2,1,0:T(8,128)(2,1)S(1)}, bf16[1,1,24,256,128]{4,3,2,1,0:T(8,128)(2,1)}, u32[]{:S(2)}) %copy-start.1) | copy-done | bytes 1572888
  17.6 28.1 %shard_map.155 = (bf16[512,128]{1,0:T(8,128)(2,1)}, f32[128,512]{1,0:T(8,128)S(1)}, bf16[9,128,512]{2,1,0:T(8,128)(2,1)S(1)}, f32[1024,128]{1,0:T(8,128)S(1)}) custom-call(s32[24]{0:T(128)S(1)} %bitcast.17, s32[1]{0:T(128)} %bitcast.9.count_ref, bf16[9,128,512]{2,1,0:T(8,128)(2,1)S(1)} %copy-done, bf16[24,256,128]{2,1,0:T(8,128)(2,1)S(1)} %bitcast.10, ...), custom_call_target="tpu_custom_call" | custom-call | tf_op jit(solution)/shard_map/pallas_call | solution.py:162
  45.8 21.5 %shard_map.156 = (f32[512,128]{1,0:T(8,128)S(1)}, f32[384,128]{1,0:T(8,128)S(1)}, f32[128,128]{1,0:T(8,128)S(1)}, f32[256,128]{1,0:T(8,128)S(1)}, f32[128,128]{1,0:T(8,128)S(1)}) custom-call(bf16[9,128,512]{2,1,0:T(8,128)(2,1)S(1)} %get-tuple-element.16.pieces_ref, f32[128,512]{1,0:T(8,128)S(1)} %get-tuple-element.17.kept_ref, ...), custom_call_target="tpu_custom_call" | custom-call | tf_op jit(solution)/shard_map/pallas_call | solution.py:360
  67.3 0.7 copy.23
  68.0 0.7 copy.24
  68.7 0.6 copy.25
  69.3 0.7 copy.26
  70.0 0.6 copy.27
Async XLA Ops:
  0.6 14.2 %copy-start.3 = (bf16[1,1,512,128]{3,2,1,0:T(8,128)(2,1)S(1)}, bf16[1,1,512,128]{3,2,1,0:T(8,128)(2,1)}, u32[]{:S(2)}) copy-start(bf16[1,1,512,128]{3,2,1,0:T(8,128)(2,1)} %param.21) | copy-start | bytes 393220
  0.6 14.2 %copy-start.7 = (bf16[128,128]{1,0:T(8,128)(2,1)S(1)}, bf16[128,128]{1,0:T(8,128)(2,1)}, u32[]{:S(2)}) copy-start(bf16[128,128]{1,0:T(8,128)(2,1)} %nw2_ref.1) | copy-start | bytes 98308
  0.7 14.2 %copy-start.5 = (bf16[256,128]{1,0:T(8,128)(2,1)S(1)}, bf16[256,128]{1,0:T(8,128)(2,1)}, u32[]{:S(2)}) copy-start(bf16[256,128]{1,0:T(8,128)(2,1)} %nw1_ref.1) | copy-start | bytes 196612
  0.7 14.2 %copy-start.6 = (bf16[128,128]{1,0:T(8,128)(2,1)S(1)}, bf16[128,128]{1,0:T(8,128)(2,1)}, u32[]{:S(2)}) copy-start(bf16[128,128]{1,0:T(8,128)(2,1)} %w2_ref.1) | copy-start | bytes 98308
  0.7 14.2 %copy-start.4 = (bf16[384,128]{1,0:T(8,128)(2,1)S(1)}, bf16[384,128]{1,0:T(8,128)(2,1)}, u32[]{:S(2)}) copy-start(bf16[384,128]{1,0:T(8,128)(2,1)} %w1_ref.1) | copy-start | bytes 294916
  0.7 14.2 %copy-start.9 = (s32[1,1,24,256]{3,2,1,0:T(8,128)S(1)}, s32[1,1,24,256]{3,2,1,0:T(8,128)}, u32[]{:S(2)}) copy-start(s32[1,1,24,256]{3,2,1,0:T(8,128)} %param.16) | copy-start | bytes 73732
  0.7 14.2 %copy-start.8 = (s32[1,1,24,256]{3,2,1,0:T(8,128)S(1)}, s32[1,1,24,256]{3,2,1,0:T(8,128)}, u32[]{:S(2)}) copy-start(s32[1,1,24,256]{3,2,1,0:T(8,128)} %param.15) | copy-start | bytes 73732
  0.7 14.2 %copy-start.10 = (s32[1,1,24]{2,1,0:T(1,128)S(1)}, s32[1,1,24]{2,1,0:T(1,128)}, u32[]{:S(2)}) copy-start(s32[1,1,24]{2,1,0:T(1,128)} %param.13) | copy-start | bytes 292
  0.7 14.2 %copy-start.2 = (bf16[1,1,512,128]{3,2,1,0:T(8,128)(2,1)S(1)}, bf16[1,1,512,128]{3,2,1,0:T(8,128)(2,1)}, u32[]{:S(2)}) copy-start(bf16[1,1,512,128]{3,2,1,0:T(8,128)(2,1)} %param.11) | copy-start | bytes 393220
  14.9 1.3 %copy-start = (bf16[9,128,512]{2,1,0:T(8,128)(2,1)S(1)}, bf16[9,128,512]{2,1,0:T(8,128)(2,1)}, u32[]{:S(2)}) copy-start(bf16[9,128,512]{2,1,0:T(8,128)(2,1)} %shard_map.154.around_ref) | copy-start | bytes 3538948
  16.2 1.4 %copy-start.1 = (bf16[1,1,24,256,128]{4,3,2,1,0:T(8,128)(2,1)S(1)}, bf16[1,1,24,256,128]{4,3,2,1,0:T(8,128)(2,1)}, u32[]{:S(2)}) copy-start(bf16[1,1,24,256,128]{4,3,2,1,0:T(8,128)(2,1)} %param.12) | copy-start | bytes 4718596

commit v3 on v2

--- a/solution.py
+++ b/solution.py
@@ -9,7 +9,7 @@
 from jax.sharding import PartitionSpec as P
 
 EPSILON = 1e-05
-UNROLL = 2
+UNROLL = 4
 
 
 def nn(a, b):
@@ -36,12 +36,17 @@
 
 
 def local_kernel(
-    factor, send_ref, count_ref, around_ref, edges_ref, sidx_ref, ridx_ref,
+    factor, send_ref, count_ref, around_hbm, edges_hbm, sidx_ref, ridx_ref,
     w1_ref, w2_ref, nw1_ref, nw2_ref, own_ref, ct_ref,
     out_ref, self_ref, piece_ref, grads_ref,
     slope_s, act_s, hat_s, inv_s, w1t_s, agg_s, gagg_s, gr_s, gs_s, g1a_s, g2_s,
+    around_ref, edges_ref, fetch_sem,
 ):
     f32, b16 = jnp.float32, jnp.bfloat16
+    fetch_around = pltpu.make_async_copy(around_hbm, around_ref, fetch_sem.at[0])
+    fetch_around.start()
+    fetch_edges = pltpu.make_async_copy(edges_hbm, edges_ref, fetch_sem.at[1])
+    fetch_edges.start()
     slots, width = sidx_ref.shape
     features, rows = around_ref.shape[1:]
     count = count_ref[0]
@@ -54,6 +59,8 @@
     gs_s[...] = jnp.zeros_like(gs_s)
     g1a_s[...] = jnp.zeros_like(g1a_s)
     g2_s[...] = jnp.zeros_like(g2_s)
+    fetch_around.wait()
+    fetch_edges.wait()
 
     def place(index_ref, step, limit):
         parts = []
@@ -161,7 +168,7 @@
     shape = jax.ShapeDtypeStruct
     return pl.pallas_call(
         functools.partial(local_kernel, factor),
-        in_specs=[smem, smem] + [vmem] * 10,
+        in_specs=[smem, smem] + [pl.BlockSpec(memory_space=pl.ANY)] * 2 + [vmem] * 8,
         out_specs=[vmem] * 4,
         out_shape=[
             shape((rows, features), b16),
@@ -181,6 +188,9 @@
             pltpu.VMEM((9, features, rows), f32),
             pltpu.VMEM((features, features), f32),
             pltpu.VMEM((features, features), f32),
+            pltpu.VMEM(around.shape, b16),
+            pltpu.VMEM(edges.shape, b16),
+            pltpu.SemaphoreType.DMA((2,)),
         ],
         compiler_params=pltpu.CompilerParams(vmem_limit_bytes=48 * 1024 * 1024),
     )(send, count, around, edges, sidx, ridx, w1, w2, nw1, nw2, own, ct)
@@ -189,26 +199,25 @@
 MESH = pl.DeviceIdType.MESH
 
 
-def neighbours():
-    p, q = lax.axis_index("gx"), lax.axis_index("gy")
-    found = []
-    for i in range(9):
-        if i != 4:
-            x, y = p + (i // 3 - 1), q + (i % 3 - 1)
-            inside = (x >= 0) & (x < lax.axis_size("gx")) & (y >= 0) & (y < lax.axis_size("gy"))
-            found.append((i, {"gx": x, "gy": y}, inside))
-    return found
+def position(slot):
+    x = lax.axis_index("gx") + (slot // 3 - 1)
+    y = lax.axis_index("gy") + (slot % 3 - 1)
+    in_x = (x >= 0) & (x < lax.axis_size("gx"))
+    in_y = (y >= 0) & (y < lax.axis_size("gy"))
+    return x, y, in_x, in_y
 
 
 def greet(extra):
     barrier = pltpu.get_barrier_semaphore()
     total = jnp.int32(len(extra))
-    for _, where, inside in neighbours():
+    for slot in (1, 3, 5, 7):
+        x, y, in_x, in_y = position(slot)
+        inside = in_x & in_y
         total = total + inside.astype(jnp.int32)
 
         @pl.when(inside)
         def _():
-            pl.semaphore_signal(barrier, inc=1, device_id=where, device_id_type=MESH)
+            pl.semaphore_signal(barrier, inc=1, device_id={"gx": x, "gy": y}, device_id_type=MESH)
 
     for where in extra:
         pl.semaphore_signal(barrier, inc=1, device_id=where, device_id_type=MESH)
@@ -222,26 +231,50 @@
     )
 
 
-def halo_kernel(own_ref, around_ref, mine_s, send_sem, recv_sem):
+def halo_kernel(own_ref, around_ref, send_sem, recv_sem):
     mine = own_ref[...].astype(jnp.float32).T.astype(jnp.bfloat16)
-    mine_s[...] = mine
     around_ref[4] = mine
+    for slot in range(9):
+        if slot != 4:
+            _, _, in_x, in_y = position(slot)
+
+            @pl.when(jnp.logical_not(in_x & in_y))
+            def _():
+                around_ref[slot] = jnp.zeros(mine.shape, mine.dtype)
+
     greet([])
-    for i, where, inside in neighbours():
-
-        @pl.when(inside)
-        def _():
-            remote(mine_s, around_ref.at[8 - i], send_sem.at[i], recv_sem.at[8 - i], where).start()
-
-        @pl.when(jnp.logical_not(inside))
-        def _():
-            around_ref[i] = jnp.zeros(mine.shape, mine.dtype)
-
-    for i, where, inside in neighbours():
-
-        @pl.when(inside)
-        def _():
-            remote(mine_s, around_ref.at[i], send_sem.at[i], recv_sem.at[i], where).wait()
+
+    def transfer(slot):
+        a, b = slot // 3, slot % 3
+        x, y, back_x, back_y = position(8 - slot)
+        _, _, in_x, in_y = position(slot)
+        if b == 1:
+            source, where, sends = 4, {"gx": x}, back_x
+        else:
+            source, where, sends = 3 * a + 1, {"gy": y}, in_x & back_y
+        copy = remote(
+            around_ref.at[source], around_ref.at[slot], send_sem.at[slot], recv_sem.at[slot], where
+        )
+        return copy, sends, in_x & in_y
+
+    copies = {slot: transfer(slot) for slot in range(9) if slot != 4}
+
+    def start(*slots):
+        for slot in slots:
+            pl.when(copies[slot][1])(copies[slot][0].start)
+
+    def arrived(*slots):
+        for slot in slots:
+            pl.when(copies[slot][2])(copies[slot][0].wait_recv)
+
+    start(1, 7, 3, 5)
+    arrived(1)
+    start(0, 2)
+    arrived(7)
+    start(6, 8)
+    arrived(3, 5, 0, 2, 6, 8)
+    for copy, sends, _ in copies.values():
+        pl.when(sends)(copy.wait_send)
 
 
 def run_halo(own):
@@ -253,7 +286,6 @@
         out_specs=vmem,
         out_shape=jax.ShapeDtypeStruct((9, features, rows), own.dtype),
         scratch_shapes=[
-            pltpu.VMEM((features, rows), own.dtype),
             pltpu.SemaphoreType.DMA((9,)),
             pltpu.SemaphoreType.DMA((9,)),
         ],
@@ -262,8 +294,8 @@
 
 
 def tail_kernel(
-    pieces_ref, kept_ref, grads_ref, node_ref, g1_ref, g2_ref, gn1_ref, gn2_ref,
-    back_s, acc_s, low_s, sum_s, low2_s, row_s, col_s, full_s,
+    pieces_ref, kept_ref, grads_ref, acc_ref, full_s,
+    back_s, pass_s, low_s, sum_s, low2_s, row_s, col_s,
     send_h, recv_h, send_r, recv_r,
 ):
     f32, b16 = jnp.float32, jnp.bfloat16
@@ -286,11 +318,30 @@
     ]
     for copy in scatter_y:
         copy.start()
-    for i, where, inside in neighbours():
-
-        @pl.when(inside)
+
+    def piece(slot):
+        a, b = slot // 3, slot % 3
+        x, y, in_x, in_y = position(slot)
+        if b == 1:
+            landing, source, where = 3 * (2 - a) + 1, pass_s.at[a], {"gx": x}
+        else:
+            landing, source, where = 3 * a + 2 - b, pieces_ref.at[slot], {"gy": y}
+        copy = remote(source, back_s.at[landing], send_h.at[slot], recv_h.at[landing], where)
+        return copy, in_x & in_y
+
+    copies = {slot: piece(slot) for slot in range(9) if slot != 4}
+
+    def take(slot):
+        @pl.when(copies[slot][1])
         def _():
-            remote(pieces_ref.at[i], back_s.at[8 - i], send_h.at[i], recv_h.at[8 - i], where).start()
+            x, y, _, _ = position(slot)
+            sender = {"gx": x} if slot % 3 == 1 else {"gy": y}
+            landed = back_s.at[slot]
+            remote(landed, landed, send_h.at[slot], recv_h.at[slot], sender).wait_recv()
+            acc_ref[...] += back_s[slot].astype(f32)
+
+    for slot in (0, 2, 6, 8, 3, 5):
+        pl.when(copies[slot][1])(copies[slot][0].start)
 
     total = grads_ref[pl.ds(pl.multiple_of(q * big, big), big), :]
     for (d, _), copy in zip(along_y, scatter_y):
@@ -304,6 +355,12 @@
     ]
     for copy in scatter_x:
         copy.start()
+    for a in (0, 2):
+        acc_ref[...] = pieces_ref[3 * a + 1].astype(f32)
+        take(3 * a)
+        take(3 * a + 2)
+        pass_s[a] = acc_ref[...].astype(b16)
+        pl.when(copies[3 * a + 1][1])(copies[3 * a + 1][0].start)
     total = sum_s[pl.ds(pl.multiple_of(p * small, small), small), :]
     for (d, _), copy in zip(along_x, scatter_x):
         copy.wait_recv()
@@ -328,25 +385,38 @@
     for copy in gather_y:
         copy.start()
 
-    acc_s[...] = kept_ref[...]
-    for i, where, inside in neighbours():
-
-        @pl.when(inside)
-        def _():
-            remote(pieces_ref.at[i], back_s.at[i], send_h.at[i], recv_h.at[i], where).wait()
-            acc_s[...] += back_s[i].astype(f32)
-
-    node_ref[...] = acc_s[...].T
+    acc_ref[...] = kept_ref[...]
+    for slot in (3, 5, 1, 7):
+        take(slot)
     for d, _ in along_y:
         source = lax.rem(q + ny - d, ny)
         theirs = rows_of(full_s, source * big, big)
         remote(theirs, theirs, send_r.at[3, d], recv_r.at[3, d], {"gy": source}).wait_recv()
-    g1_ref[...] = full_s[: 3 * features].astype(f32)
-    g2_ref[...] = full_s[3 * features : 4 * features].astype(f32)
-    gn1_ref[...] = full_s[4 * features : 6 * features].astype(f32)
-    gn2_ref[...] = full_s[6 * features : 7 * features].astype(f32)
     for copy in scatter_y + scatter_x + gather_y:
         copy.wait_send()
+    for copy, sends in copies.values():
+        pl.when(sends)(copy.wait_send)
+
+
+def finish_kernel(acc_ref, full_ref, node_ref, g1_ref, g2_ref, gn1_ref, gn2_ref):
+    node_ref[...] = acc_ref[...].T
+    first = 0
+    for ref in (g1_ref, g2_ref, gn1_ref, gn2_ref):
+        ref[...] = full_ref[first : first + ref.shape[0]].astype(jnp.float32)
+        first += ref.shape[0]
+
+
+def run_finish(acc, full):
+    features, rows = acc.shape
+    vmem = pl.BlockSpec(memory_space=pltpu.VMEM)
+    shape = jax.ShapeDtypeStruct
+    return pl.pallas_call(
+        finish_kernel,
+        in_specs=[vmem] * 2,
+        out_specs=[vmem] * 5,
+        out_shape=[shape((rows, features), jnp.float32)]
+        + [shape((n * features, features), jnp.float32) for n in (3, 1, 2, 1)],
+    )(acc, full)
 
 
 def run_tail(pieces, kept, grads):
@@ -360,18 +430,16 @@
     return pl.pallas_call(
         tail_kernel,
         in_specs=[vmem] * 3,
-        out_specs=[vmem] * 5,
-        out_shape=[shape((rows, features), f32)]
-        + [shape((n * features, features), f32) for n in (3, 1, 2, 1)],
+        out_specs=[vmem] * 2,
+        out_shape=[shape((features, rows), f32), shape((padded, features), b16)],
         scratch_shapes=[
             pltpu.VMEM((9, features, rows), b16),
-            pltpu.VMEM((features, rows), f32),
+            pltpu.VMEM((3, features, rows), b16),
             pltpu.VMEM((padded, features), b16),
             pltpu.VMEM((big, features), f32),
             pltpu.VMEM((big, features), b16),
             pltpu.VMEM((ny, big, features), b16),
             pltpu.VMEM((nx, small, features), b16),
-            pltpu.VMEM((padded, features), b16),
             pltpu.SemaphoreType.DMA((9,)),
             pltpu.SemaphoreType.DMA((9,)),
             pltpu.SemaphoreType.DMA((4, max(nx, ny))),
@@ -425,7 +493,7 @@
         edge_send[0, 0], edge_recv[0, 0], edge_w1, edge_w2, node_w1, node_w2, own, node_ct[0, 0],
     )
     if direct:
-        node_grad, *summed = run_tail(pieces, kept, grads)
+        node_grad, *summed = run_finish(*run_tail(pieces, kept, grads))
     else:
         node_grad = return_permute(pieces, kept)
         grads = lax.psum(grads, ("gx", "gy"))

time: 71.4 us -> 59.7 us (0.84)
  Pallas kernels: 63 us -> 53.8 us
  local copies, waits for them, and re-layouts: 6 us -> 4.1 us
    pallas_call x1, Pallas kernels: 28.1 us -> 15.5 us  [run_local(): pl.pallas_call(functools.partial(local_kernel, factor), in_specs=[smem, s...]
    pallas_call x1 -> x2, Pallas kernels: 21.5 us -> 24.3 us  [the longest x1 22.4 us: run_tail(): pl.pallas_call(tail_kernel, in_specs=[vmem] * 3, out_specs=[vmem] * 2, ou...]
    unnamed x27 -> x26, local copies, waits for them, and re-layouts: 6 us -> 4.1 us
where the time goes in v3:
time: 59.7 us; the launch traced here: 59.5 us
  Pallas kernels  53.8 us (90%)
  local copies, waits for them, and re-layouts  4.1 us (7%)
  between operations  1.59 us (3%)
    pallas_call x1, Pallas kernels, run_tail(): pl.pallas_call(tail_kernel, in_specs=[vmem] * 3, out_specs=[vmem] * 2, ou...  22.4 us
    pallas_call x1, Pallas kernels, run_local(): pl.pallas_call(functools.partial(local_kernel, factor), in_specs=[smem, s...  15.5 us
    pallas_call x1, Pallas kernels, run_halo(): pl.pallas_call(halo_kernel, in_specs=[vmem], out_specs=vmem, out_shape=ja...  13.9 us
    unnamed x26, local copies, waits for them, and re-layouts  4.1 us
    pallas_call x1, Pallas kernels, run_finish(): pl.pallas_call(finish_kernel, in_specs=[vmem] * 2, out_specs=[vmem] * 5,...  1.95 us

profile of v3, /device:TPU:1, one launch (start us, length us, event | category | flops | bytes accessed | tf_op | source)
XLA Modules:
  0.0 59.5 jit_solution(13138753174781239911)
XLA Ops:
  0.6 0.0 copy-start.5
  0.6 0.0 copy-start.9
  0.7 0.0 copy-start.7
  0.7 0.0 copy-start.8
  0.7 0.0 copy-start.6
  0.7 0.0 copy-start.11
  0.7 0.0 copy-start.10
  0.7 0.0 copy-start.12
  0.7 0.0 copy-start.2
  1.5 13.9 %shard_map.154.around_hbm = bf16[9,128,512]{2,1,0:T(8,128)(2,1)} custom-call(bf16[512,128]{1,0:T(8,128)(2,1)} %bitcast.11), custom_call_target="tpu_custom_call" | custom-call | tf_op jit(solution)/shard_map/pallas_call | solution.py:283
  15.4 0.0 copy-done.5
  15.4 0.0 copy-done.9
  15.4 0.0 copy-done.7
  15.4 0.0 copy-done.8
  15.4 0.0 copy-done.6
  15.5 0.0 copy-done.11
  15.5 0.0 copy-done.10
  15.5 0.0 copy-done.12
  15.5 0.0 copy-done.2
  15.5 0.0 copy-start
  15.5 1.3 %copy-done = bf16[9,128,512]{2,1,0:T(8,128)(2,1)S(1)} copy-done((bf16[9,128,512]{2,1,0:T(8,128)(2,1)S(1)}, bf16[9,128,512]{2,1,0:T(8,128)(2,1)}, u32[]{:S(2)}) %copy-start) | copy-done | bytes 1179672
  16.8 0.0 copy-start.1
  16.8 1.4 %copy-done.1 = bf16[1,1,24,256,128]{4,3,2,1,0:T(8,128)(2,1)S(1)} copy-done((bf16[1,1,24,256,128]{4,3,2,1,0:T(8,128)(2,1)S(1)}, bf16[1,1,24,256,128]{4,3,2,1,0:T(8,128)(2,1)}, u32[]{:S(2)}) %copy-start.1) | copy-done | bytes 1572888
  18.2 15.5 %shard_map.155 = (bf16[512,128]{1,0:T(8,128)(2,1)}, f32[128,512]{1,0:T(8,128)S(1)}, bf16[9,128,512]{2,1,0:T(8,128)(2,1)S(1)}, f32[1024,128]{1,0:T(8,128)S(1)}) custom-call(s32[24]{0:T(128)S(1)} %bitcast.16, s32[1]{0:T(128)} %bitcast.9.count_ref, bf16[9,128,512]{2,1,0:T(8,128)(2,1)S(1)} %copy-done, bf16[24,256,128]{2,1,0:T(8,128)(2,1)S(1)} %bitcast.10, ...), custom_call_target="tpu_custom_call" | custom-call | tf_op jit(solution)/shard_map/pallas_call | solution.py:169
  33.7 22.4 %shard_map.156 = (f32[128,512]{1,0:T(8,128)S(1)}, bf16[1024,128]{1,0:T(8,128)(2,1)S(1)}) custom-call(bf16[9,128,512]{2,1,0:T(8,128)(2,1)S(1)} %get-tuple-element.18.pieces_ref, f32[128,512]{1,0:T(8,128)S(1)} %get-tuple-element.19.kept_ref, f32[1024,128]{1,0:T(8,128)S(1)} %get-tuple-element.20.grads_ref), custom_call_target="tpu_custom_call" | custom-call | tf_op jit(solution)/shard_map/pallas_call | solution.py:430
  56.1 0.0 copy-start.3
  56.1 0.7 %copy-done.3 = f32[128,512]{1,0:T(8,128)} copy-done((f32[128,512]{1,0:T(8,128)}, f32[128,512]{1,0:T(8,128)S(1)}, u32[]{:S(2)}) %copy-start.3) | copy-done | bytes 262168
  56.8 0.0 copy-start.4
  56.8 0.7 %copy-done.4 = bf16[1024,128]{1,0:T(8,128)(2,1)} copy-done((bf16[1024,128]{1,0:T(8,128)(2,1)}, bf16[1024,128]{1,0:T(8,128)(2,1)S(1)}, u32[]{:S(2)}) %copy-start.4) | copy-done | bytes 262168
  57.5 2.0 %shard_map.157 = (f32[512,128]{1,0:T(8,128)}, f32[384,128]{1,0:T(8,128)}, f32[128,128]{1,0:T(8,128)}, f32[256,128]{1,0:T(8,128)}, f32[128,128]{1,0:T(8,128)}) custom-call(f32[128,512]{1,0:T(8,128)} %copy-done.3, bf16[1024,128]{1,0:T(8,128)(2,1)} %copy-done.4), custom_call_target="tpu_custom_call" | custom-call | tf_op jit(solution)/shard_map/pallas_call | solution.py:413
Async XLA Ops:
  0.6 14.8 %copy-start.5 = (bf16[1,1,512,128]{3,2,1,0:T(8,128)(2,1)S(1)}, bf16[1,1,512,128]{3,2,1,0:T(8,128)(2,1)}, u32[]{:S(2)}) copy-start(bf16[1,1,512,128]{3,2,1,0:T(8,128)(2,1)} %param.21) | copy-start | bytes 393220
  0.6 14.8 %copy-start.9 = (bf16[128,128]{1,0:T(8,128)(2,1)S(1)}, bf16[128,128]{1,0:T(8,128)(2,1)}, u32[]{:S(2)}) copy-start(bf16[128,128]{1,0:T(8,128)(2,1)} %nw2_ref.1) | copy-start | bytes 98308
  0.7 14.8 %copy-start.7 = (bf16[256,128]{1,0:T(8,128)(2,1)S(1)}, bf16[256,128]{1,0:T(8,128)(2,1)}, u32[]{:S(2)}) copy-start(bf16[256,128]{1,0:T(8,128)(2,1)} %nw1_ref.1) | copy-start | bytes 196612
  0.7 14.8 %copy-start.8 = (bf16[128,128]{1,0:T(8,128)(2,1)S(1)}, bf16[128,128]{1,0:T(8,128)(2,1)}, u32[]{:S(2)}) copy-start(bf16[128,128]{1,0:T(8,128)(2,1)} %w2_ref.1) | copy-start | bytes 98308
  0.7 14.8 %copy-start.6 = (bf16[384,128]{1,0:T(8,128)(2,1)S(1)}, bf16[384,128]{1,0:T(8,128)(2,1)}, u32[]{:S(2)}) copy-start(bf16[384,128]{1,0:T(8,128)(2,1)} %w1_ref.1) | copy-start | bytes 294916
  0.7 14.8 %copy-start.11 = (s32[1,1,24,256]{3,2,1,0:T(8,128)S(1)}, s32[1,1,24,256]{3,2,1,0:T(8,128)}, u32[]{:S(2)}) copy-start(s32[1,1,24,256]{3,2,1,0:T(8,128)} %param.16) | copy-start | bytes 73732
  0.7 14.8 %copy-start.10 = (s32[1,1,24,256]{3,2,1,0:T(8,128)S(1)}, s32[1,1,24,256]{3,2,1,0:T(8,128)}, u32[]{:S(2)}) copy-start(s32[1,1,24,256]{3,2,1,0:T(8,128)} %param.15) | copy-start | bytes 73732
  0.7 14.8 %copy-start.12 = (s32[1,1,24]{2,1,0:T(1,128)S(1)}, s32[1,1,24]{2,1,0:T(1,128)}, u32[]{:S(2)}) copy-start(s32[1,1,24]{2,1,0:T(1,128)} %param.13) | copy-start | bytes 292
  0.7 14.8 %copy-start.2 = (bf16[1,1,512,128]{3,2,1,0:T(8,128)(2,1)S(1)}, bf16[1,1,512,128]{3,2,1,0:T(8,128)(2,1)}, u32[]{:S(2)}) copy-start(bf16[1,1,512,128]{3,2,1,0:T(8,128)(2,1)} %param.11) | copy-start | bytes 393220
  15.5 1.3 %copy-start = (bf16[9,128,512]{2,1,0:T(8,128)(2,1)S(1)}, bf16[9,128,512]{2,1,0:T(8,128)(2,1)}, u32[]{:S(2)}) copy-start(bf16[9,128,512]{2,1,0:T(8,128)(2,1)} %shard_map.154.around_hbm) | copy-start | bytes 3538948
  16.8 1.4 %copy-start.1 = (bf16[1,1,24,256,128]{4,3,2,1,0:T(8,128)(2,1)S(1)}, bf16[1,1,24,256,128]{4,3,2,1,0:T(8,128)(2,1)}, u32[]{:S(2)}) copy-start(bf16[1,1,24,256,128]{4,3,2,1,0:T(8,128)(2,1)} %param.12) | copy-start | bytes 4718596
  56.1 0.7 %copy-start.3 = (f32[128,512]{1,0:T(8,128)}, f32[128,512]{1,0:T(8,128)S(1)}, u32[]{:S(2)}) copy-start(f32[128,512]{1,0:T(8,128)S(1)} %get-tuple-element.21.acc_ref) | copy-start | bytes 786436
  56.8 0.7 %copy-start.4 = (bf16[1024,128]{1,0:T(8,128)(2,1)}, bf16[1024,128]{1,0:T(8,128)(2,1)S(1)}, u32[]{:S(2)}) copy-start(bf16[1024,128]{1,0:T(8,128)(2,1)S(1)} %get-tuple-element.22.full_ref) | copy-start | bytes 786436

commit v4 on v3

--- a/solution.py
+++ b/solution.py
@@ -9,7 +9,7 @@
 from jax.sharding import PartitionSpec as P
 
 EPSILON = 1e-05
-UNROLL = 4
+UNROLL = 6
 
 
 def nn(a, b):
@@ -71,8 +71,9 @@
                 index = jnp.where(k < count, index, rows)
             parts.append(index)
         index = jnp.concatenate(parts, axis=1)
-        spot = lax.broadcasted_iota(jnp.int32, (rows, UNROLL * width), 0)
-        return (spot == index).astype(f32).astype(b16)
+        spot = lax.broadcasted_iota(jnp.int16, (rows, UNROLL * width), 0)
+        match = spot == index.astype(jnp.int16)
+        return jnp.where(match, jnp.ones((), b16), jnp.zeros((), b16))
 
     def forward(step, carry):
         at_recv = place(ridx_ref, step, True)
@@ -192,7 +193,7 @@
             pltpu.VMEM(edges.shape, b16),
             pltpu.SemaphoreType.DMA((2,)),
         ],
-        compiler_params=pltpu.CompilerParams(vmem_limit_bytes=48 * 1024 * 1024),
+        compiler_params=pltpu.CompilerParams(vmem_limit_bytes=60 * 1024 * 1024),
     )(send, count, around, edges, sidx, ridx, w1, w2, nw1, nw2, own, ct)
 
 
@@ -340,9 +341,6 @@
             remote(landed, landed, send_h.at[slot], recv_h.at[slot], sender).wait_recv()
             acc_ref[...] += back_s[slot].astype(f32)
 
-    for slot in (0, 2, 6, 8, 3, 5):
-        pl.when(copies[slot][1])(copies[slot][0].start)
-
     total = grads_ref[pl.ds(pl.multiple_of(q * big, big), big), :]
     for (d, _), copy in zip(along_y, scatter_y):
         copy.wait_recv()
@@ -355,12 +353,8 @@
     ]
     for copy in scatter_x:
         copy.start()
-    for a in (0, 2):
-        acc_ref[...] = pieces_ref[3 * a + 1].astype(f32)
-        take(3 * a)
-        take(3 * a + 2)
-        pass_s[a] = acc_ref[...].astype(b16)
-        pl.when(copies[3 * a + 1][1])(copies[3 * a + 1][0].start)
+    for slot in (0, 2, 6, 8, 3, 5):
+        pl.when(copies[slot][1])(copies[slot][0].start)
     total = sum_s[pl.ds(pl.multiple_of(p * small, small), small), :]
     for (d, _), copy in zip(along_x, scatter_x):
         copy.wait_recv()
@@ -372,6 +366,12 @@
     ]
     for copy in gather_x:
         copy.start()
+    for a in (0, 2):
+        acc_ref[...] = pieces_ref[3 * a + 1].astype(f32)
+        take(3 * a)
+        take(3 * a + 2)
+        pass_s[a] = acc_ref[...].astype(b16)
+        pl.when(copies[3 * a + 1][1])(copies[3 * a + 1][0].start)
     for d, _ in along_x:
         source = lax.rem(p + nx - d, nx)
         theirs = rows_of(full_s, q * big + source * small, small)
@@ -398,7 +398,15 @@
         pl.when(sends)(copy.wait_send)
 
 
-def finish_kernel(acc_ref, full_ref, node_ref, g1_ref, g2_ref, gn1_ref, gn2_ref):
+def finish_kernel(
+    acc_hbm, full_hbm, node_ref, g1_ref, g2_ref, gn1_ref, gn2_ref, acc_ref, full_ref, fetch_sem
+):
+    fetch_acc = pltpu.make_async_copy(acc_hbm, acc_ref, fetch_sem.at[0])
+    fetch_acc.start()
+    fetch_full = pltpu.make_async_copy(full_hbm, full_ref, fetch_sem.at[1])
+    fetch_full.start()
+    fetch_acc.wait()
+    fetch_full.wait()
     node_ref[...] = acc_ref[...].T
     first = 0
     for ref in (g1_ref, g2_ref, gn1_ref, gn2_ref):
@@ -412,10 +420,16 @@
     shape = jax.ShapeDtypeStruct
     return pl.pallas_call(
         finish_kernel,
-        in_specs=[vmem] * 2,
+        in_specs=[pl.BlockSpec(memory_space=pl.ANY)] * 2,
         out_specs=[vmem] * 5,
         out_shape=[shape((rows, features), jnp.float32)]
         + [shape((n * features, features), jnp.float32) for n in (3, 1, 2, 1)],
+        scratch_shapes=[
+            pltpu.VMEM(acc.shape, acc.dtype),
+            pltpu.VMEM(full.shape, full.dtype),
+            pltpu.SemaphoreType.DMA((2,)),
+        ],
+        compiler_params=pltpu.CompilerParams(vmem_limit_bytes=60 * 1024 * 1024),
     )(acc, full)
 
 

time: 59.7 us -> 59.4 us (level)
    pallas_call x1, Pallas kernels: 22.4 us -> 16.5 us  [run_tail(): pl.pallas_call(tail_kernel, in_specs=[vmem] * 3, out_specs=[vmem] * 2, ou...]
    pallas_call x1, Pallas kernels: 15.5 us -> 21.2 us  [run_local(): pl.pallas_call(functools.partial(local_kernel, factor), in_specs=[smem, s...]
    unnamed x26 -> x10, local copies, waits for them, and re-layouts: 4.1 us -> 4.64 us
where the time goes in v4:
time: 59.4 us; the launch traced here: 59.5 us
  Pallas kernels  53.5 us (90%)
  local copies, waits for them, and re-layouts  4.64 us (8%)
  between operations  1.32 us (2%)
    pallas_call x1, Pallas kernels, run_local(): pl.pallas_call(functools.partial(local_kernel, factor), in_specs=[smem, s...  21.2 us
    pallas_call x1, Pallas kernels, run_tail(): pl.pallas_call(tail_kernel, in_specs=[vmem] * 3, out_specs=[vmem] * 2, ou...  16.5 us
    pallas_call x1, Pallas kernels, run_halo(): pl.pallas_call(halo_kernel, in_specs=[vmem], out_specs=vmem, out_shape=ja...  13.9 us
    unnamed x10, local copies, waits for them, and re-layouts  4.64 us
    pallas_call x1, Pallas kernels, run_finish(): pl.pallas_call(finish_kernel, in_specs=[pl.BlockSpec(memory_space=pl.ANY)...  1.97 us

profile of v4, /device:TPU:1, one launch (start us, length us, event | category | flops | bytes accessed | tf_op | source)
XLA Modules:
  0.0 59.5 jit_solution(3057647214029005185)
XLA Ops:
  1.3 13.9 %shard_map.154.around_hbm = bf16[9,128,512]{2,1,0:T(8,128)(2,1)} custom-call(bf16[512,128]{1,0:T(8,128)(2,1)} %bitcast.11), custom_call_target="tpu_custom_call" | custom-call | tf_op jit(solution)/shard_map/pallas_call | solution.py:284
  15.2 21.2 %shard_map.155 = (bf16[512,128]{1,0:T(8,128)(2,1)}, f32[128,512]{1,0:T(8,128)}, bf16[9,128,512]{2,1,0:T(8,128)(2,1)}, f32[1024,128]{1,0:T(8,128)}) custom-call(s32[24]{0:T(128)} %bitcast.16, s32[1]{0:T(128)} %bitcast.9.count_ref, bf16[9,128,512]{2,1,0:T(8,128)(2,1)} %shard_map.154.around_hbm, bf16[24,256,128]{2,1,0:T(8,128)(2,1)} %bitcast.10, ...), custom_call_target="tpu_custom_call" | custom-call | tf_op jit(solution)/shard_map/pallas_call | solution.py:170
  36.3 0.0 copy-start
  36.3 1.3 %copy-done = bf16[9,128,512]{2,1,0:T(8,128)(2,1)S(1)} copy-done((bf16[9,128,512]{2,1,0:T(8,128)(2,1)S(1)}, bf16[9,128,512]{2,1,0:T(8,128)(2,1)}, u32[]{:S(2)}) %copy-start) | copy-done | bytes 1179672
  37.6 0.0 copy-start.1
  37.6 1.0 %copy-done.1 = f32[1024,128]{1,0:T(8,128)S(1)} copy-done((f32[1024,128]{1,0:T(8,128)S(1)}, f32[1024,128]{1,0:T(8,128)}, u32[]{:S(2)}) %copy-start.1) | copy-done | bytes 524312
  38.6 0.0 copy-start.2
  38.6 0.9 %copy-done.2 = f32[128,512]{1,0:T(8,128)S(1)} copy-done((f32[128,512]{1,0:T(8,128)S(1)}, f32[128,512]{1,0:T(8,128)}, u32[]{:S(2)}) %copy-start.2) | copy-done | bytes 262168
  39.6 16.5 %shard_map.156 = (f32[128,512]{1,0:T(8,128)S(1)}, bf16[1024,128]{1,0:T(8,128)(2,1)S(1)}) custom-call(bf16[9,128,512]{2,1,0:T(8,128)(2,1)S(1)} %copy-done, f32[128,512]{1,0:T(8,128)S(1)} %copy-done.2, f32[1024,128]{1,0:T(8,128)S(1)} %copy-done.1), custom_call_target="tpu_custom_call" | custom-call | tf_op jit(solution)/shard_map/pallas_call | solution.py:444
  56.1 0.0 copy-start.3
  56.1 0.7 %copy-done.3 = f32[128,512]{1,0:T(8,128)} copy-done((f32[128,512]{1,0:T(8,128)}, f32[128,512]{1,0:T(8,128)S(1)}, u32[]{:S(2)}) %copy-start.3) | copy-done | bytes 262168
  56.8 0.0 copy-start.4
  56.8 0.7 %copy-done.4 = bf16[1024,128]{1,0:T(8,128)(2,1)} copy-done((bf16[1024,128]{1,0:T(8,128)(2,1)}, bf16[1024,128]{1,0:T(8,128)(2,1)S(1)}, u32[]{:S(2)}) %copy-start.4) | copy-done | bytes 262168
  57.5 2.0 %shard_map.157 = (f32[512,128]{1,0:T(8,128)}, f32[384,128]{1,0:T(8,128)}, f32[128,128]{1,0:T(8,128)}, f32[256,128]{1,0:T(8,128)}, f32[128,128]{1,0:T(8,128)}) custom-call(f32[128,512]{1,0:T(8,128)} %copy-done.3, bf16[1024,128]{1,0:T(8,128)(2,1)} %copy-done.4), custom_call_target="tpu_custom_call" | custom-call | tf_op jit(solution)/shard_map/pallas_call | solution.py:421
Async XLA Ops:
  36.3 1.3 %copy-start = (bf16[9,128,512]{2,1,0:T(8,128)(2,1)S(1)}, bf16[9,128,512]{2,1,0:T(8,128)(2,1)}, u32[]{:S(2)}) copy-start(bf16[9,128,512]{2,1,0:T(8,128)(2,1)} %get-tuple-element.18.pieces_ref) | copy-start | bytes 3538948
  37.6 1.0 %copy-start.1 = (f32[1024,128]{1,0:T(8,128)S(1)}, f32[1024,128]{1,0:T(8,128)}, u32[]{:S(2)}) copy-start(f32[1024,128]{1,0:T(8,128)} %get-tuple-element.20.grads_ref) | copy-start | bytes 1572868
  38.6 0.9 %copy-start.2 = (f32[128,512]{1,0:T(8,128)S(1)}, f32[128,512]{1,0:T(8,128)}, u32[]{:S(2)}) copy-start(f32[128,512]{1,0:T(8,128)} %get-tuple-element.19.kept_ref) | copy-start | bytes 786436
  56.1 0.7 %copy-start.3 = (f32[128,512]{1,0:T(8,128)}, f32[128,512]{1,0:T(8,128)S(1)}, u32[]{:S(2)}) copy-start(f32[128,512]{1,0:T(8,128)S(1)} %get-tuple-element.21.acc_hbm) | copy-start | bytes 786436
  56.8 0.7 %copy-start.4 = (bf16[1024,128]{1,0:T(8,128)(2,1)}, bf16[1024,128]{1,0:T(8,128)(2,1)S(1)}, u32[]{:S(2)}) copy-start(bf16[1024,128]{1,0:T(8,128)(2,1)S(1)} %get-tuple-element.22.full_hbm) | copy-start | bytes 786436

commit v5 on v4

--- a/solution.py
+++ b/solution.py
@@ -295,18 +295,28 @@
 
 
 def tail_kernel(
-    pieces_ref, kept_ref, grads_ref, acc_ref, full_s,
+    pieces_ref, kept_hbm, grads_hbm, acc_ref, full_s,
     back_s, pass_s, low_s, sum_s, low2_s, row_s, col_s,
-    send_h, recv_h, send_r, recv_r,
+    send_h, recv_h, send_r, recv_r, kept_ref, grads_ref, middle_s, fetch_sem,
 ):
+    fetch_grads = pltpu.make_async_copy(grads_hbm, grads_ref, fetch_sem.at[0])
+    fetch_grads.start()
+    fetches = [
+        pltpu.make_async_copy(kept_hbm, kept_ref, fetch_sem.at[1]),
+        pltpu.make_async_copy(pieces_ref.at[1], middle_s.at[0], fetch_sem.at[2]),
+        pltpu.make_async_copy(pieces_ref.at[7], middle_s.at[2], fetch_sem.at[3]),
+    ]
+    for fetch in fetches:
+        fetch.start()
     f32, b16 = jnp.float32, jnp.bfloat16
     p, q = lax.axis_index("gx"), lax.axis_index("gy")
     nx, ny = lax.axis_size("gx"), lax.axis_size("gy")
-    padded, features = grads_ref.shape
+    padded, features = grads_hbm.shape
     big, small = padded // ny, padded // (nx * ny)
     along_y = [(d, lax.rem(q + d, ny)) for d in range(1, ny)]
     along_x = [(d, lax.rem(p + d, nx)) for d in range(1, nx)]
 
+    fetch_grads.wait()
     low_s[...] = grads_ref[...].astype(b16)
     greet([{"gy": y} for _, y in along_y] + [{"gx": x} for _, x in along_x])
 
@@ -366,8 +376,10 @@
     ]
     for copy in gather_x:
         copy.start()
+    for fetch in fetches:
+        fetch.wait()
     for a in (0, 2):
-        acc_ref[...] = pieces_ref[3 * a + 1].astype(f32)
+        acc_ref[...] = middle_s[a].astype(f32)
         take(3 * a)
         take(3 * a + 2)
         pass_s[a] = acc_ref[...].astype(b16)
@@ -443,7 +455,7 @@
     shape = jax.ShapeDtypeStruct
     return pl.pallas_call(
         tail_kernel,
-        in_specs=[vmem] * 3,
+        in_specs=[pl.BlockSpec(memory_space=pl.ANY)] * 3,
         out_specs=[vmem] * 2,
         out_shape=[shape((features, rows), f32), shape((padded, features), b16)],
         scratch_shapes=[
@@ -458,9 +470,13 @@
             pltpu.SemaphoreType.DMA((9,)),
             pltpu.SemaphoreType.DMA((4, max(nx, ny))),
             pltpu.SemaphoreType.DMA((4, max(nx, ny))),
+            pltpu.VMEM((features, rows), f32),
+            pltpu.VMEM((padded, features), f32),
+            pltpu.VMEM((3, features, rows), b16),
+            pltpu.SemaphoreType.DMA((4,)),
         ],
         compiler_params=pltpu.CompilerParams(
-            collective_id=1, has_side_effects=True, vmem_limit_bytes=32 * 1024 * 1024
+            collective_id=1, has_side_effects=True, vmem_limit_bytes=63 * 1024 * 1024
         ),
     )(pieces, kept, grads)
 

time: 59.4 us -> 56.9 us (0.958)
  local copies, waits for them, and re-layouts: 4.64 us -> 0 us
  Pallas kernels: 53.5 us -> 55.3 us
    pallas_call x1, Pallas kernels: 16.5 us -> 22.1 us  [run_tail(): pl.pallas_call(tail_kernel, in_specs=[pl.BlockSpec(memory_space=pl.ANY)]...]
    unnamed x10 -> x0, local copies, waits for them, and re-layouts: 4.64 us -> none
    pallas_call x1, Pallas kernels: 21.2 us -> 17.4 us  [run_local(): pl.pallas_call(functools.partial(local_kernel, factor), in_specs=[smem, s...]
where the time goes in v5:
time: 56.9 us; the launch traced here: 56.6 us
  Pallas kernels  55.3 us (97%)
  between operations  1.3 us (2%)
    pallas_call x1, Pallas kernels, run_tail(): pl.pallas_call(tail_kernel, in_specs=[pl.BlockSpec(memory_space=pl.ANY)]...  22.1 us
    pallas_call x1, Pallas kernels, run_local(): pl.pallas_call(functools.partial(local_kernel, factor), in_specs=[smem, s...  17.4 us
    pallas_call x1, Pallas kernels, run_halo(): pl.pallas_call(halo_kernel, in_specs=[vmem], out_specs=vmem, out_shape=ja...  13.9 us
    pallas_call x1, Pallas kernels, run_finish(): pl.pallas_call(finish_kernel, in_specs=[pl.BlockSpec(memory_space=pl.ANY)...  1.97 us

profile of v5, /device:TPU:1, one launch (start us, length us, event | category | flops | bytes accessed | tf_op | source)
XLA Modules:
  0.0 56.6 jit_solution(14914231064172319768)
XLA Ops:
  1.3 13.9 %shard_map.154.around_hbm = bf16[9,128,512]{2,1,0:T(8,128)(2,1)} custom-call(bf16[512,128]{1,0:T(8,128)(2,1)} %bitcast.11), custom_call_target="tpu_custom_call" | custom-call | tf_op jit(solution)/shard_map/pallas_call | solution.py:284
  15.2 17.4 %shard_map.155 = (bf16[512,128]{1,0:T(8,128)(2,1)}, f32[128,512]{1,0:T(8,128)}, bf16[9,128,512]{2,1,0:T(8,128)(2,1)}, f32[1024,128]{1,0:T(8,128)}) custom-call(s32[24]{0:T(128)} %bitcast.16, s32[1]{0:T(128)} %bitcast.9.count_ref, bf16[9,128,512]{2,1,0:T(8,128)(2,1)} %shard_map.154.around_hbm, bf16[24,256,128]{2,1,0:T(8,128)(2,1)} %bitcast.10, ...), custom_call_target="tpu_custom_call" | custom-call | tf_op jit(solution)/shard_map/pallas_call | solution.py:170
  32.6 22.1 %shard_map.156 = (f32[128,512]{1,0:T(8,128)}, bf16[1024,128]{1,0:T(8,128)(2,1)}) custom-call(bf16[9,128,512]{2,1,0:T(8,128)(2,1)} %get-tuple-element.18.pieces_ref, f32[128,512]{1,0:T(8,128)} %get-tuple-element.19.kept_hbm, f32[1024,128]{1,0:T(8,128)} %get-tuple-element.20.grads_hbm), custom_call_target="tpu_custom_call" | custom-call | tf_op jit(solution)/shard_map/pallas_call | solution.py:456
  54.7 2.0 %shard_map.157 = (f32[512,128]{1,0:T(8,128)}, f32[384,128]{1,0:T(8,128)}, f32[128,128]{1,0:T(8,128)}, f32[256,128]{1,0:T(8,128)}, f32[128,128]{1,0:T(8,128)}) custom-call(f32[128,512]{1,0:T(8,128)} %get-tuple-element.21.acc_hbm, bf16[1024,128]{1,0:T(8,128)(2,1)} %get-tuple-element.22.full_hbm), custom_call_target="tpu_custom_call" | custom-call | tf_op jit(solution)/shard_map/pallas_call | solution.py:433
